TPU v7x, 256 devices: a whole 4x4x8 slice. The times are simulated.
256 devices in a mesh: frames: 8 (over z_lo, y), patch: 32 (over x, z_hi, core).
Axes of the slice: x: 4, y: 4, z: 8 (z_hi: 4, z_lo: 2; z = z_hi * 2 + z_lo), core: 2. Of those that a mesh axis runs over, the one named last changes fastest.
Arguments:
- object_band: float32 [2048, 256], P('patch'), may hold values from -6 to 6
- data_band: float32 [2048, 16, 256], P('patch', 'frames'), may hold values from -6 to 6
- coeffs: float32 [16, 32, 4, 200], P('frames', 'patch'), may hold values from -5 to 5
- mode_basis: float32 [200, 2304], replicated, may hold values from -0.4375 to 0.4375
- offsets: int32 [32, 4, 2], P('patch'), may hold values from 0 to 16
- window_ids: int32 [32, 4], P('patch'), may hold values from 0 to 3
- counts: int32 [32], P('patch'), may hold values from 2 to 4, as said below
Outputs:
- object_grad: float32 [2048, 256], P('patch')
- coeff_grad: float32 [16, 32, 4, 200], P('frames', 'patch')
Inputs may be any that keep to these rules, and one draw needn't show every extreme that they name: Patch row r holds its first counts[r] patches inside the image; some patch row holds all 4 and some only 2.
All inputs are finite; a program needn't handle non-finite values.
Results may differ from a plain program's by a relative error of at most 0.0003.
Values sent between devices are 32-bit elements; how exact they have to be, the bound alone decides.
No kernel may reach another device: no remote copies, remote signals or barrier semaphores. Data moves between devices by JAX's collectives and lax.ppermute only.
A program may use at most 64 MiB of HBM per device.

v0:
```python
import math

import jax
import jax.numpy as jnp
import ml_dtypes
import numpy as np
from jax import lax
from jax.experimental import pallas as pl
from jax.experimental.pallas import tpu as pltpu
from jax.sharding import PartitionSpec as P

PP = 96
PU = 48
STRIDE = 64
HALO = 24
PC = 4
FK = 2
NI = PC * FK
LANES = 128
MODES = 200
TALL = PP + 8
HEIGHT = STRIDE + 2 * HALO + 8
F32 = jnp.float32
BF16 = jnp.bfloat16
VMEM_LIMIT = 56 * 1024 * 1024


def halves(matrix):
    high = matrix.astype(ml_dtypes.bfloat16)
    low = (matrix - high.astype(np.float64)).astype(ml_dtypes.bfloat16)
    return high, low


def dft(points, length):
    turns = np.outer(np.arange(points), np.arange(length)) % points
    angles = 2.0 * math.pi / points * turns
    return np.cos(angles), -np.sin(angles)


def constants():
    full_re, full_im = dft(PP, PP)
    half_re, half_im = dft(PP, PU)
    fwd_right = np.zeros((256, 256))
    fwd_right[:96, :96] = full_re
    fwd_right[128:224, :96] = -full_im
    fwd_right[:96, 128:224] = full_im
    fwd_right[128:224, 128:224] = full_re
    inv_right = np.zeros((256, 256))
    inv_right[:96, :96] = full_re
    inv_right[128:224, :96] = full_im
    inv_right[:96, 128:224] = -full_im
    inv_right[128:224, 128:224] = full_re
    pupil_right = np.zeros((128, 256))
    pupil_right[:48, :96] = half_re.T
    pupil_right[64:112, :96] = -half_im.T
    pupil_right[:48, 128:224] = half_im.T
    pupil_right[64:112, 128:224] = half_re.T
    pupil_left = np.block([[half_re, -half_im], [half_im, half_re]])
    fwd_left = np.block([[full_re, -full_im], [full_im, full_re]])
    inv_left = np.block([[full_re, full_im], [-full_im, full_re]])
    real_left = np.concatenate([full_re, full_im], axis=0)

    def stack(matrix):
        return np.concatenate(halves(matrix), axis=0)

    def twice(matrix):
        high, low = halves(matrix)
        return np.concatenate([high, low], axis=1)

    side = np.arange(PP) + 0.5
    windows = np.zeros((4, PP, LANES), np.float32)
    for kind in range(4):
        edge = float(max(PP * (kind + 1) // 12, 1))
        rising = 0.5 - 0.5 * np.cos(math.pi * np.minimum(side, edge) / edge)
        profile = rising * rising[::-1]
        windows[kind, :, :PP] = np.outer(profile, profile)
    centre = np.arange(PU) + 0.5 - 0.5 * PU
    opening = (centre[:, None] ** 2 + centre[None, :] ** 2 <= (0.5 * PU) ** 2).reshape(1, PU * PU)
    return {
        "fwd_right": stack(fwd_right),
        "inv_right": stack(inv_right),
        "pupil_right": stack(pupil_right),
        "pupil_left": twice(pupil_left),
        "fwd_left": stack(fwd_left),
        "inv_left": stack(inv_left),
        "real_left": twice(real_left),
        "part_left": stack(inv_left[:PP]),
        "back_left": stack(pupil_left.T.copy()),
        "back_right": stack(pupil_right.T.copy()),
        "windows": windows,
        "opening": opening.astype(np.float32),
    }


def split(values):
    high = values.astype(BF16)
    return high, (values - high.astype(F32)).astype(BF16)


def mm(a, b):
    return jnp.dot(a, b, preferred_element_type=F32)


def right(values, matrix_ref):
    depth = matrix_ref.shape[0] // 2
    rows = values.shape[0]
    high, low = split(values)
    both = mm(jnp.concatenate([high, low], axis=0), matrix_ref[:depth])
    return both[:rows] + both[rows:] + mm(high, matrix_ref[depth:])


def left(matrix_ref, values):
    rows = matrix_ref.shape[0] // 2
    high, low = split(values)
    both = mm(matrix_ref[...], high)
    return both[:rows] + both[rows:] + mm(matrix_ref[:rows], low)


def left_wide(matrix_ref, values):
    depth = values.shape[0]
    high, low = split(values)
    return mm(matrix_ref[...], jnp.concatenate([high, high], axis=0)) + mm(matrix_ref[:, :depth], low)


def to_rows(spectrum):
    parts = []
    for c in range(PC):
        lanes = slice(c * LANES, (c + 1) * LANES)
        parts.append(jnp.concatenate([spectrum[:PP, lanes], spectrum[PP:, lanes]], axis=1))
    return jnp.concatenate(parts, axis=0)


def to_lanes(rows):
    re = jnp.concatenate([rows[c * PP : (c + 1) * PP, :LANES] for c in range(PC)], axis=1)
    im = jnp.concatenate([rows[c * PP : (c + 1) * PP, LANES:] for c in range(PC)], axis=1)
    return jnp.concatenate([re, im], axis=0)


def sin_cos(angle):
    turns = jnp.floor(angle * (2.0 / math.pi) + 0.5)
    rest = angle - turns * 1.5703125
    rest = rest - turns * 4.837512969970703125e-4
    rest = rest - turns * 7.54978995489188216e-8
    sq = rest * rest
    sine = ((-1.9515295891e-4 * sq + 8.3321608736e-3) * sq - 1.6666654611e-1) * sq * rest + rest
    cosine = ((2.443315711809948e-5 * sq - 1.388731625493765e-3) * sq + 4.166664568298827e-2) * sq * sq - 0.5 * sq + 1.0
    quarter = turns.astype(jnp.int32) & 3
    swapped = (quarter & 1) == 1
    sin_now = jnp.where(swapped, cosine, sine)
    cos_now = jnp.where(swapped, sine, cosine)
    sin_now = jnp.where(quarter >= 2, -sin_now, sin_now)
    cos_now = jnp.where((quarter == 1) | (quarter == 2), -cos_now, cos_now)
    return sin_now, cos_now


def pack_kernel(object_ref, data_ref, on_ref, off_ref):
    even = lax.axis_index("patch") % 2 == 0
    low, high = STRIDE - HALO, 0
    on_at = pl.multiple_of(jnp.where(even, low, high), 8)
    off_at = pl.multiple_of(jnp.where(even, high, low), 8)
    for ref, at in ((on_ref, on_at), (off_ref, off_at)):
        ref[0:HALO, :] = object_ref[pl.ds(at, HALO), :]
        for k in range(FK):
            ref[(k + 1) * HALO : (k + 2) * HALO, :] = data_ref[pl.ds(at, HALO), k, :]


def psf_kernel(coeffs_ref, basis_ref, opening_ref, pr_ref, pl_ref, fl_ref, fr_ref,
               pupil_ref, field_ref, spec_ref, scale_ref, rows_scr, left_scr):
    coeffs = jnp.concatenate([coeffs_ref[0, 0], coeffs_ref[1, 0]], axis=0)
    c_high = coeffs.astype(BF16)
    rest = coeffs - c_high.astype(F32)
    c_mid = rest.astype(BF16)
    c_low = (rest - c_mid.astype(F32)).astype(BF16)
    basis = basis_ref[...]
    b_high = basis.astype(BF16)
    b_rest = basis - b_high.astype(F32)
    b_mid = b_rest.astype(BF16)
    b_low = (b_rest - b_mid.astype(F32)).astype(BF16)
    wave = (mm(c_high, b_low) + mm(c_mid, b_mid) + mm(c_low, b_high)) + (mm(c_high, b_mid) + mm(c_mid, b_high)) + mm(c_high, b_high)
    sine, cosine = sin_cos(wave)
    opening = opening_ref[...]
    re = cosine * opening
    im = sine * opening
    pupil_ref[...] = jnp.zeros_like(pupil_ref)
    for a in range(PU):
        pupil_ref[a * NI : (a + 1) * NI, 0:PU] = re[:, a * PU : (a + 1) * PU]
        pupil_ref[a * NI : (a + 1) * NI, 64 : 64 + PU] = im[:, a * PU : (a + 1) * PU]
    mixed = right(pupil_ref[...], pr_ref)
    rows_scr[0] = mixed[:, :LANES]
    rows_scr[1] = mixed[:, LANES:]
    for n in range(NI):
        lanes = slice(n * LANES, (n + 1) * LANES)
        left_scr[0:PU, lanes] = rows_scr[0, pl.ds(n, PU, stride=NI), :]
        left_scr[PU:, lanes] = rows_scr[1, pl.ds(n, PU, stride=NI), :]
    field = left_wide(pl_ref, left_scr[...])
    field_ref[...] = field
    intensity = field[:PP] * field[:PP] + field[PP:] * field[PP:]
    sums = jnp.concatenate(
        [jnp.sum(intensity[:, n * LANES : (n + 1) * LANES], axis=0, keepdims=True) for n in range(NI)], axis=0
    )
    scale = 1.0 / jnp.sum(sums, axis=1, keepdims=True)
    scale_ref[...] = jnp.broadcast_to(scale, (NI, LANES))
    spread = jnp.concatenate(
        [intensity[:, n * LANES : (n + 1) * LANES] * scale[n : n + 1, :] for n in range(NI)], axis=1
    )
    pair = jnp.concatenate([spread[:, : PC * LANES], spread[:, PC * LANES :]], axis=0)
    spec_ref[...] = right(to_rows(left(fl_ref, pair)), fr_ref)


def misfit_kernel(offsets_ref, kinds_ref, counts_ref, object_ref, data_ref, on_ref, off_ref, spec_ref, windows_ref,
                  rl_ref, fl_ref, fr_ref, ir_ref, il_ref, gl_ref,
                  obj_spec_ref, res_spec_ref, centre_ref, on_rim_ref, off_rim_ref, ext, total):
    even = lax.axis_index("patch") % 2 == 0
    on_at = pl.multiple_of(jnp.where(even, STRIDE + HALO, 0), 8)
    off_at = pl.multiple_of(jnp.where(even, 0, STRIDE + HALO), 8)
    edge = jnp.zeros((HEIGHT, LANES), F32)
    mid = slice(LANES, 3 * LANES)
    for i in range(1 + FK):
        ext[i, :, 0:LANES] = edge
        ext[i, :, 3 * LANES :] = edge
        ext[i, STRIDE + 2 * HALO :, mid] = jnp.zeros((HEIGHT - STRIDE - 2 * HALO, 2 * LANES), F32)
        ext[i, HALO : HALO + STRIDE, mid] = object_ref[...] if i == 0 else data_ref[:, i - 1, :]
        ext[i, pl.ds(on_at, HALO), mid] = on_ref[i * HALO : (i + 1) * HALO, :]
        ext[i, pl.ds(off_at, HALO), mid] = off_ref[i * HALO : (i + 1) * HALO, :]

    row_base = [pl.multiple_of((offsets_ref[0, c, 0] >> 3) << 3, 8) for c in range(PC)]
    row_rest = [offsets_ref[0, c, 0] & 7 for c in range(PC)]
    base = [0, LANES, LANES, 2 * LANES]
    shift = [LANES + c * STRIDE - HALO - base[c] + offsets_ref[0, c, 1] for c in range(PC)]

    def cut(i, c):
        block = ext[i, pl.ds(row_base[c], TALL), base[c] : base[c] + 2 * LANES]
        moved = pltpu.roll(block, 2 * LANES - shift[c], 1)[:, :LANES]
        return pltpu.roll(moved, jnp.where(row_rest[c] == 0, 0, TALL - row_rest[c]), 0)[:PP]

    windows = [windows_ref[kinds_ref[0, c]] for c in range(PC)]
    weighted = jnp.concatenate([windows[c] * cut(0, c) for c in range(PC)], axis=1)
    obj = right(to_rows(left_wide(rl_ref, weighted)), fr_ref)
    obj_spec_ref[...] = obj
    spec = spec_ref[...]
    o_re, o_im, s_re, s_im = obj[:, :LANES], obj[:, LANES:], spec[:, :LANES], spec[:, LANES:]
    product = jnp.concatenate([o_re * s_re - o_im * s_im, o_re * s_im + o_im * s_re], axis=1)
    predicted = left(il_ref, to_lanes(right(product, ir_ref)))
    parts = []
    for k in range(FK):
        for c in range(PC):
            usable = jnp.where(c < counts_ref[0], 1.0, 0.0).astype(F32)
            lanes = slice(c * LANES, (c + 1) * LANES)
            here = predicted[k * PP : (k + 1) * PP, lanes] * (1.0 / (PP * PP))
            parts.append((here - windows[c] * cut(k + 1, c)) * usable)
    residual = jnp.concatenate([jnp.concatenate(parts[k * PC : (k + 1) * PC], axis=1) for k in range(FK)], axis=0)
    res = right(to_rows(left(fl_ref, residual)), fr_ref)
    res_spec_ref[...] = res
    r_re, r_im = res[:, :LANES], res[:, LANES:]
    back = jnp.concatenate([s_re * r_re + s_im * r_im, s_re * r_im - s_im * r_re], axis=1)
    grad = left(gl_ref, to_lanes(right(back, ir_ref)))
    total[...] = jnp.zeros_like(total)
    for c in range(PC):
        mine = windows[c] * grad[:, c * LANES : (c + 1) * LANES] * (1.0 / (PP * PP))
        mine = pltpu.roll(jnp.concatenate([mine, jnp.zeros((TALL - PP, LANES), F32)], axis=0), row_rest[c], 0)
        placed = pltpu.roll(jnp.concatenate([mine, jnp.zeros((TALL, LANES), F32)], axis=1), shift[c], 1)
        rows, lanes = pl.ds(row_base[c], TALL), slice(base[c], base[c] + 2 * LANES)
        total[rows, lanes] = total[rows, lanes] + placed
    centre_ref[...] = total[HALO : HALO + STRIDE, mid]
    on_rim_ref[...] = total[pl.ds(on_at, HALO), mid]
    off_rim_ref[...] = total[pl.ds(off_at, HALO), mid]


def mode_kernel(obj_spec_ref, res_spec_ref, field_ref, scale_ref, pupil_ref, basis_ref, ir_ref, il_ref, bl_ref, br_ref,
                out_ref, rows_scr, flat_scr):
    obj, res = obj_spec_ref[...], res_spec_ref[...]
    o_re, o_im, r_re, r_im = obj[:, :LANES], obj[:, LANES:], res[:, :LANES], res[:, LANES:]
    back = jnp.concatenate([o_re * r_re + o_im * r_im, o_re * r_im - o_im * r_re], axis=1)
    grad = left(il_ref, to_lanes(right(back, ir_ref)))
    re_parts, im_parts = [], []
    for n in range(NI):
        k, c = divmod(n, PC)
        lanes = slice(n * LANES, (n + 1) * LANES)
        f_re, f_im = field_ref[:PP, lanes], field_ref[PP:, lanes]
        scale = scale_ref[n : n + 1, :]
        spread = (f_re * f_re + f_im * f_im) * scale
        mine = grad[k * PP : (k + 1) * PP, c * LANES : (c + 1) * LANES] * (1.0 / (PP * PP))
        mean = jnp.sum(jnp.sum(mine * spread, axis=0, keepdims=True), axis=1, keepdims=True)
        slope = 2.0 * scale * (mine - mean)
        re_parts.append(f_re * slope)
        im_parts.append(f_im * slope)
    wide = jnp.concatenate([jnp.concatenate(re_parts, axis=1), jnp.concatenate(im_parts, axis=1)], axis=0)
    half = left(bl_ref, wide)
    for n in range(NI):
        lanes = slice(n * LANES, (n + 1) * LANES)
        rows_scr[0, pl.ds(n, PU, stride=NI), :] = half[:PU, lanes]
        rows_scr[1, pl.ds(n, PU, stride=NI), :] = half[PU:, lanes]
    pupil_grad = right(jnp.concatenate([rows_scr[0], rows_scr[1]], axis=1), br_ref)
    pupil = pupil_ref[...]
    crossed = pupil * pltpu.roll(pupil_grad, 64, 1)
    slopes = crossed - pltpu.roll(crossed, 64, 1)
    for a in range(PU):
        flat_scr[:, a * PU : (a + 1) * PU] = slopes[a * NI : (a + 1) * NI, 0:PU]
    high, low = split(flat_scr[...])
    b_high, b_low = split(basis_ref[...])

    def by_modes(a, b):
        return lax.dot_general(a, b, (((1,), (1,)), ((), ())), preferred_element_type=F32)

    both = by_modes(jnp.concatenate([high, low], axis=0), b_high)
    out = both[:NI] + both[NI:] + by_modes(high, b_low)
    out_ref[0, 0] = out[:PC]
    out_ref[1, 0] = out[PC:]


def call(kernel, out_shapes, scratch=(), smem=0, inputs=0, name=None):
    vmem = pl.BlockSpec(memory_space=pltpu.VMEM)
    return pl.pallas_call(
        kernel,
        out_shape=out_shapes,
        in_specs=[pl.BlockSpec(memory_space=pltpu.SMEM)] * smem + [vmem] * inputs,
        out_specs=jax.tree.map(lambda _: vmem, out_shapes),
        scratch_shapes=list(scratch),
        compiler_params=pltpu.CompilerParams(vmem_limit_bytes=VMEM_LIMIT),
        name=name,
    )


def shape(*dims):
    return jax.ShapeDtypeStruct(dims, F32)


def swap_on(values):
    count = lax.axis_size("patch")
    return lax.ppermute(values, "patch", [(i, i ^ 1) for i in range(count)])


def swap_off(values):
    count = lax.axis_size("patch")
    pairs = [(i, i + 1) for i in range(1, count - 1, 2)]
    return lax.ppermute(values, "patch", pairs + [(j, i) for i, j in pairs])


def swap_frames(values, bit):
    count = lax.axis_size("frames")
    return lax.ppermute(values, "frames", [(i, i ^ bit) for i in range(count)])


def body(object_band, data_band, coeffs, mode_basis, offsets, window_ids, counts):
    columns = object_band.shape[1]
    const = {name: jnp.asarray(value) for name, value in constants().items()}
    on_send, off_send = call(pack_kernel, [shape(3 * HALO, columns)] * 2, inputs=2, name="pack")(object_band, data_band)
    off_halo = swap_off(off_send)
    on_halo = swap_on(on_send)
    pupil, field, spec, scale = call(
        psf_kernel,
        [shape(PU * NI, LANES), shape(2 * PP, NI * LANES), shape(PC * PP, 2 * LANES), shape(NI, LANES)],
        scratch=[pltpu.VMEM((2, PU * NI, LANES), F32), pltpu.VMEM((2 * PU, NI * LANES), F32)],
        inputs=7,
        name="psf",
    )(coeffs, mode_basis, const["opening"], const["pupil_right"], const["pupil_left"], const["fwd_left"], const["fwd_right"])
    obj_spec, res_spec, centre, on_rim, off_rim = call(
        misfit_kernel,
        [shape(PC * PP, 2 * LANES)] * 2 + [shape(STRIDE, columns), shape(HALO, columns), shape(HALO, columns)],
        scratch=[pltpu.VMEM((1 + FK, HEIGHT, 4 * LANES), F32), pltpu.VMEM((HEIGHT, 4 * LANES), F32)],
        smem=3,
        inputs=12,
        name="misfit",
    )(
        offsets, window_ids, counts, object_band, data_band, on_halo, off_halo, spec, const["windows"],
        const["real_left"], const["fwd_left"], const["fwd_right"], const["inv_right"], const["inv_left"], const["part_left"],
    )
    on_rim = swap_on(on_rim)
    off_rim = swap_off(off_rim)
    even = lax.axis_index("patch") % 2 == 0
    upper = jnp.where(even, off_rim, on_rim)
    lower = jnp.where(even, on_rim, off_rim)
    rows = jnp.concatenate([centre[:HALO] + upper, centre[HALO : STRIDE - HALO], centre[STRIDE - HALO :] + lower], axis=0)
    for bit in (4, 1, 2):
        rows = rows + swap_frames(rows, bit)
    coeff_grad = call(
        mode_kernel,
        shape(FK, 1, PC, MODES),
        scratch=[pltpu.VMEM((2, PU * NI, LANES), F32), pltpu.VMEM((NI, PU * PU), F32)],
        inputs=10,
        name="modes",
    )(
        obj_spec, res_spec, field, scale, pupil, mode_basis,
        const["inv_right"], const["inv_left"], const["back_left"], const["back_right"],
    )
    return rows, coeff_grad


def solution(mesh):
    in_specs = (
        P("patch", None),
        P("patch", "frames", None),
        P("frames", "patch", None, None),
        P(),
        P("patch", None, None),
        P("patch", None),
        P("patch"),
    )
    out_specs = (P("patch", None), P("frames", "patch", None, None))
    return jax.shard_map(body, mesh=mesh, in_specs=in_specs, out_specs=out_specs, check_vma=False)
```

profile of v0, /device:TPU:6, one launch (start us, length us, event | category | flops | bytes accessed | tf_op | source)
XLA Modules:
  0.0 51.1 jit_solution(9107182333337249875)
XLA Ops:
  0.6 1.6 %pack.1 = (f32[72,256]{1,0:T(8,128)}, f32[72,256]{1,0:T(8,128)}) custom-call(f32[64,256]{1,0:T(8,128)} %object_ref.3, f32[64,2,256]{2,1,0:T(2,128)} %data_ref.3), custom_call_target="tpu_custom_call" | custom-call | tf_op jit(solution)/shard_map/pack/pallas_call | solution.py:347
  2.3 0.0 collective-permute-start
  2.3 8.6 %collective-permute-start.1 = (f32[72,256]{1,0:T(8,128)}, f32[72,256]{1,0:T(8,128)S(1)}, u32[]{:S(2)}, u32[]{:S(2)}) collective-permute-start(f32[72,256]{1,0:T(8,128)} %get-tuple-element.14), channel_id=1, source_target_pairs={{1,2},{3,4},{5,6},{7,8},{9,10},{11,12},{13,14},{15,16},{17,18},{19... | collective-permute-start | bytes 221192 | tf_op jit(solution)/shard_map/ppermute | solution.py:336
  10.9 1.3 %copy.21.offsets_ref = s32[1,4,2]{2,1,0:T(4,128)} copy(s32[1,4,2]{1,2,0:T(2,128)} %param.23) | data formatting | bytes 64 | tf_op args[4]
  12.9 5.1 %psf.1 = (f32[384,128]{1,0:T(8,128)}, f32[192,1024]{1,0:T(8,128)}, f32[384,256]{1,0:T(8,128)}, f32[8,128]{1,0:T(8,128)}) custom-call(f32[2,1,4,200]{3,2,1,0:T(4,128)} %coeffs_ref.1, f32[200,2304]{1,0:T(8,128)} %basis_ref.3, f32[1,2304]{1,0:T(1,128)} %constant.53.clone.opening_ref, bf16[256,256]{1,0:T(8,128)(2,1)} %constant.44.clone.pr_ref, ...), custom_call_target="tpu_custom_call" | custom-call | tf_op jit(solution)/shard_map/psf/pallas_call | solution.py:350
  18.0 0.0 collective-permute-done.on_ref
  18.0 0.0 copy-start
  18.0 0.0 collective-permute-done.1.off_ref
  18.0 0.0 copy-start.1
  18.0 0.6 %copy-done = f32[72,256]{1,0:T(8,128)} copy-done((f32[72,256]{1,0:T(8,128)}, f32[72,256]{1,0:T(8,128)S(1)}, u32[]{:S(2)}) %copy-start) | copy-done | bytes 73752
  18.6 0.0 copy-done.1
  18.6 5.2 %misfit.1 = (f32[384,256]{1,0:T(8,128)}, f32[384,256]{1,0:T(8,128)}, f32[64,256]{1,0:T(8,128)}, f32[24,256]{1,0:T(8,128)}, f32[24,256]{1,0:T(8,128)}) custom-call(s32[1,4,2]{2,1,0:T(4,128)} %copy.21.offsets_ref, s32[1,4]{1,0:T(1,128)} %kinds_ref.1, s32[1]{0:T(128)S(6)} %copy.22.counts_ref, f32[64,256]{1,0:T(8,128)} %object_ref.3, f32[64,2,256]{2,1,0:T(2,128)} %data_ref.3, ...), custom_call_target="tpu_custom_call" | custom-call | tf_op jit(solution)/shard_map/misfit/pallas_call | solution.py:357
  23.9 2.5 %collective-permute-start.2 = (f32[24,256]{1,0:T(8,128)}, f32[24,256]{1,0:T(8,128)S(1)}, u32[]{:S(2)}, u32[]{:S(2)}) collective-permute-start(f32[24,256]{1,0:T(8,128)} %get-tuple-element.17), channel_id=1, source_target_pairs={{1,2},{3,4},{5,6},{7,8},{9,10},{11,12},{13,14},{15,16},{17,18},{19... | collective-permute-start | bytes 73736 | tf_op jit(solution)/shard_map/ppermute | solution.py:336
  26.4 0.1 collective-permute-start.3
  26.5 0.7 %slice.10 = f32[16,256]{1,0:T(8,128)S(1)} slice(f32[64,256]{1,0:T(8,128)} %get-tuple-element.16), slice={[24:40], [0:256]} | slice | bytes 32768 | tf_op jit(solution)/shard_map/slice | solution.py:373
  27.2 5.0 %collective-permute-done.2 = f32[24,256]{1,0:T(8,128)S(1)} collective-permute-done((f32[24,256]{1,0:T(8,128)}, f32[24,256]{1,0:T(8,128)S(1)}, u32[]{:S(2)}, u32[]{:S(2)}) %collective-permute-start.2) | collective-permute-done | bytes 24608 | tf_op jit(solution)/shard_map/ppermute | solution.py:336
  32.3 0.0 collective-permute-done.3
  32.3 0.8 %select_add_fusion.1 = (f32[24,256]{1,0:T(8,128)S(1)}, f32[24,256]{1,0:T(8,128)S(1)}) fusion(f32[24,256]{1,0:T(8,128)S(1)} %collective-permute-done.2, f32[24,256]{1,0:T(8,128)S(1)} %collective-permute-done.3, f32[64,256]{1,0:T(8,128)} %get-tuple-element.16, pred[]{:T(512)S(6)} %eq.5), kind=kLoop, calls=%fused_computation.2 | loop fusion | flops 24576 | bytes 147457 | tf_op jit(solution)/shard_map/add | solution.py:373
  33.0 1.2 %collective-permute-start.4 = (f32[64,256]{1,0:T(8,128)S(1)}, f32[64,256]{1,0:T(8,128)S(1)}, u32[]{:S(2)}, u32[]{:S(2)}) collective-permute-start(f32[64,256]{1,0:T(8,128)S(1)} %pad_maximum_fusion), channel_id=1, source_target_pairs={{0,128},{32,160},{64,192},{96,224},{128,0},{160,32},{192,64},{224,... | collective-permute-start | bytes 196616 | tf_op jit(solution)/shard_map/ppermute | solution.py:341
  34.2 3.1 %collective-permute-done.4 = f32[64,256]{1,0:T(8,128)S(1)} collective-permute-done((f32[64,256]{1,0:T(8,128)S(1)}, f32[64,256]{1,0:T(8,128)S(1)}, u32[]{:S(2)}, u32[]{:S(2)}) %collective-permute-start.4) | collective-permute-done | bytes 65568 | tf_op jit(solution)/shard_map/ppermute | solution.py:341
  37.4 1.7 %collective-permute-start.5 = (f32[64,256]{1,0:T(8,128)S(1)}, f32[64,256]{1,0:T(8,128)S(1)}, u32[]{:S(2)}, u32[]{:S(2)}) collective-permute-start(f32[64,256]{1,0:T(8,128)S(1)} %fusion), channel_id=1, source_target_pairs={{0,32},{32,0},{64,96},{96,64},{128,160},{160,128},{192,224},{224,1... | collective-permute-start | bytes 196616 | tf_op jit(solution)/shard_map/ppermute | solution.py:341
  39.1 2.7 %collective-permute-done.5 = f32[64,256]{1,0:T(8,128)S(1)} collective-permute-done((f32[64,256]{1,0:T(8,128)S(1)}, f32[64,256]{1,0:T(8,128)S(1)}, u32[]{:S(2)}, u32[]{:S(2)}) %collective-permute-start.5) | collective-permute-done | bytes 65568 | tf_op jit(solution)/shard_map/ppermute | solution.py:341
  41.8 3.3 %collective-permute-start.6 = (f32[64,256]{1,0:T(8,128)S(1)}, f32[64,256]{1,0:T(8,128)S(1)}, u32[]{:S(2)}, u32[]{:S(2)}) collective-permute-start(f32[64,256]{1,0:T(8,128)S(1)} %add.23), channel_id=1, source_target_pairs={{0,64},{32,96},{64,0},{96,32},{128,192},{160,224},{192,128},{224,1... | collective-permute-start | bytes 196616 | tf_op jit(solution)/shard_map/ppermute | solution.py:341
  45.0 5.4 %modes.1 = f32[2,1,4,200]{3,2,1,0:T(4,128)} custom-call(f32[384,256]{1,0:T(8,128)} %get-tuple-element.19.obj_spec_ref, f32[384,256]{1,0:T(8,128)} %get-tuple-element.20.res_spec_ref, f32[192,1024]{1,0:T(8,128)} %get-tuple-element.21.field_ref, f32[8,128]{1,0:T(8,128)} %get-tuple-element.22.scale_ref, f32[384,128]{1,0:T(8,128)} %get-tuple-element.23.pupil_ref, ...), custom_call_target="tpu_custom_call" | custom-call | tf_op jit(solution)/shard_map/modes/pallas_call | solution.py:376
  50.4 0.0 collective-permute-done.6
  50.5 0.6 %add.24 = f32[64,256]{1,0:T(8,128)} add(f32[64,256]{1,0:T(8,128)S(1)} %add.23, f32[64,256]{1,0:T(8,128)S(1)} %collective-permute-done.6) | non-fusion elementwise | flops 16384 | bytes 196608 | tf_op jit(solution)/shard_map/add | solution.py:375
  (3 shorter events, 0.0 us)
Async XLA Ops:
  2.3 15.7 %collective-permute-start = (f32[72,256]{1,0:T(8,128)}, f32[72,256]{1,0:T(8,128)S(1)}, u32[]{:S(2)}, u32[]{:S(2)}) collective-permute-start(f32[72,256]{1,0:T(8,128)} %get-tuple-element.13), channel_id=1, source_target_pairs={{0,1},{1,0},{2,3},{3,2},{4,5},{5,4},{6,7},{7,6},{8,9},{9,8},{10,11... | collective-permute-start | bytes 221192 | tf_op jit(solution)/shard_map/ppermute | solution.py:330
  2.3 15.7 %collective-permute-start.1 = (f32[72,256]{1,0:T(8,128)}, f32[72,256]{1,0:T(8,128)S(1)}, u32[]{:S(2)}, u32[]{:S(2)}) collective-permute-start(f32[72,256]{1,0:T(8,128)} %get-tuple-element.14), channel_id=1, source_target_pairs={{1,2},{3,4},{5,6},{7,8},{9,10},{11,12},{13,14},{15,16},{17,18},{19... | collective-permute-start | bytes 221192 | tf_op jit(solution)/shard_map/ppermute | solution.py:336
  18.0 0.6 %copy-start = (f32[72,256]{1,0:T(8,128)}, f32[72,256]{1,0:T(8,128)S(1)}, u32[]{:S(2)}) copy-start(f32[72,256]{1,0:T(8,128)S(1)} %collective-permute-done.on_ref) | copy-start | bytes 221188
  18.0 0.6 %copy-start.1 = (f32[72,256]{1,0:T(8,128)}, f32[72,256]{1,0:T(8,128)S(1)}, u32[]{:S(2)}) copy-start(f32[72,256]{1,0:T(8,128)S(1)} %collective-permute-done.1.off_ref) | copy-start | bytes 221188
  23.9 8.4 %collective-permute-start.2 = (f32[24,256]{1,0:T(8,128)}, f32[24,256]{1,0:T(8,128)S(1)}, u32[]{:S(2)}, u32[]{:S(2)}) collective-permute-start(f32[24,256]{1,0:T(8,128)} %get-tuple-element.17), channel_id=1, source_target_pairs={{1,2},{3,4},{5,6},{7,8},{9,10},{11,12},{13,14},{15,16},{17,18},{19... | collective-permute-start | bytes 73736 | tf_op jit(solution)/shard_map/ppermute | solution.py:336
  26.4 5.9 %collective-permute-start.3 = (f32[24,256]{1,0:T(8,128)}, f32[24,256]{1,0:T(8,128)S(1)}, u32[]{:S(2)}, u32[]{:S(2)}) collective-permute-start(f32[24,256]{1,0:T(8,128)} %get-tuple-element.18), channel_id=1, source_target_pairs={{0,1},{1,0},{2,3},{3,2},{4,5},{5,4},{6,7},{7,6},{8,9},{9,8},{10,11... | collective-permute-start | bytes 73736 | tf_op jit(solution)/shard_map/ppermute | solution.py:330
  33.0 4.4 %collective-permute-start.4 = (f32[64,256]{1,0:T(8,128)S(1)}, f32[64,256]{1,0:T(8,128)S(1)}, u32[]{:S(2)}, u32[]{:S(2)}) collective-permute-start(f32[64,256]{1,0:T(8,128)S(1)} %pad_maximum_fusion), channel_id=1, source_target_pairs={{0,128},{32,160},{64,192},{96,224},{128,0},{160,32},{192,64},{224,... | collective-permute-start | bytes 196616 | tf_op jit(solution)/shard_map/ppermute | solution.py:341
  37.4 4.4 %collective-permute-start.5 = (f32[64,256]{1,0:T(8,128)S(1)}, f32[64,256]{1,0:T(8,128)S(1)}, u32[]{:S(2)}, u32[]{:S(2)}) collective-permute-start(f32[64,256]{1,0:T(8,128)S(1)} %fusion), channel_id=1, source_target_pairs={{0,32},{32,0},{64,96},{96,64},{128,160},{160,128},{192,224},{224,1... | collective-permute-start | bytes 196616 | tf_op jit(solution)/shard_map/ppermute | solution.py:341
  41.8 8.7 %collective-permute-start.6 = (f32[64,256]{1,0:T(8,128)S(1)}, f32[64,256]{1,0:T(8,128)S(1)}, u32[]{:S(2)}, u32[]{:S(2)}) collective-permute-start(f32[64,256]{1,0:T(8,128)S(1)} %add.23), channel_id=1, source_target_pairs={{0,64},{32,96},{64,0},{96,32},{128,192},{160,224},{192,128},{224,1... | collective-permute-start | bytes 196616 | tf_op jit(solution)/shard_map/ppermute | solution.py:341
where the time goes:
time: 51.4 us; the launch traced here: 51.1 us
  Pallas kernels  17.4 us (34%)
  starting transfers between devices  17.3 us (34%)
  waiting for transfers between devices  10.9 us (21%)
  local copies, waits for them, and re-layouts  2.7 us (5%)
  other arithmetic  1.43 us (3%)
  between operations  1.35 us (3%)
    ppermute x2, starting transfers between devices, swap_off(): return lax.ppermute(values, 'patch', pairs + [(j, i) for i, j in pairs])  11.1 us
    ppermute x3, starting transfers between devices, swap_frames(): return lax.ppermute(values, 'frames', [(i, i ^ bit) for i in range(count)])  6.15 us
    ppermute x3, waiting for transfers between devices, swap_frames(): return lax.ppermute(values, 'frames', [(i, i ^ bit) for i in range(count)])  5.83 us
    pallas_call x1, Pallas kernels, body(): call(mode_kernel, shape(FK, 1, PC, MODES), scratch=[pltpu.VMEM((2, PU * N...  5.41 us
    pallas_call x1, Pallas kernels, body(): call(misfit_kernel, [shape(PC * PP, 2 * LANES)] * 2 + [shape(STRIDE, colu...  5.24 us
    pallas_call x1, Pallas kernels, body(): call(psf_kernel, [shape(PU * NI, LANES), shape(2 * PP, NI * LANES), shape...  5.13 us
    ppermute x2, waiting for transfers between devices, swap_off(): return lax.ppermute(values, 'patch', pairs + [(j, i) for i, j in pairs])  5.02 us
    unnamed x5, local copies, waits for them, and re-layouts  1.97 us
  transfers between devices with their start and end apart: 7, of which 3 were waited for; matrix products, arithmetic and copies ran while one was open for 4% of the time, Pallas kernels for 21%

commit v1 on v0

--- a/solution.py
+++ b/solution.py
@@ -22,7 +22,9 @@
 HEIGHT = STRIDE + 2 * HALO + 8
 F32 = jnp.float32
 BF16 = jnp.bfloat16
-VMEM_LIMIT = 56 * 1024 * 1024
+VMEM_LIMIT = 8 * 1024 * 1024
+CHUNK = 768
+CHUNKS = PU * PU // CHUNK
 
 
 def halves(matrix):
@@ -45,11 +47,6 @@
     fwd_right[128:224, :96] = -full_im
     fwd_right[:96, 128:224] = full_im
     fwd_right[128:224, 128:224] = full_re
-    inv_right = np.zeros((256, 256))
-    inv_right[:96, :96] = full_re
-    inv_right[128:224, :96] = full_im
-    inv_right[:96, 128:224] = -full_im
-    inv_right[128:224, 128:224] = full_re
     pupil_right = np.zeros((128, 256))
     pupil_right[:48, :96] = half_re.T
     pupil_right[64:112, :96] = -half_im.T
@@ -57,7 +54,6 @@
     pupil_right[64:112, 128:224] = half_re.T
     pupil_left = np.block([[half_re, -half_im], [half_im, half_re]])
     fwd_left = np.block([[full_re, -full_im], [full_im, full_re]])
-    inv_left = np.block([[full_re, full_im], [-full_im, full_re]])
     real_left = np.concatenate([full_re, full_im], axis=0)
 
     def stack(matrix):
@@ -78,13 +74,10 @@
     opening = (centre[:, None] ** 2 + centre[None, :] ** 2 <= (0.5 * PU) ** 2).reshape(1, PU * PU)
     return {
         "fwd_right": stack(fwd_right),
-        "inv_right": stack(inv_right),
         "pupil_right": stack(pupil_right),
         "pupil_left": twice(pupil_left),
         "fwd_left": stack(fwd_left),
-        "inv_left": stack(inv_left),
         "real_left": twice(real_left),
-        "part_left": stack(inv_left[:PP]),
         "back_left": stack(pupil_left.T.copy()),
         "back_right": stack(pupil_right.T.copy()),
         "windows": windows,
@@ -114,6 +107,13 @@
     high, low = split(values)
     both = mm(matrix_ref[...], high)
     return both[:rows] + both[rows:] + mm(matrix_ref[:rows], low)
+
+
+def left_part(matrix_ref, values):
+    rows = matrix_ref.shape[0] // 2
+    half = rows // 2
+    high, low = split(values)
+    return mm(matrix_ref[:half], high) + mm(matrix_ref[rows : rows + half], high) + mm(matrix_ref[:half], low)
 
 
 def left_wide(matrix_ref, values):
@@ -153,38 +153,89 @@
     return sin_now, cos_now
 
 
-def pack_kernel(object_ref, data_ref, on_ref, off_ref):
+def fetch(pairs, sems):
+    copies = [pltpu.make_async_copy(src, dst, sems.at[i]) for i, (src, dst) in enumerate(pairs)]
+    for copy in copies:
+        copy.start()
+    return copies
+
+
+def pack_kernel(object_hbm, data_hbm, on_ref, off_ref, on_scr, off_scr, sems):
     even = lax.axis_index("patch") % 2 == 0
     low, high = STRIDE - HALO, 0
     on_at = pl.multiple_of(jnp.where(even, low, high), 8)
     off_at = pl.multiple_of(jnp.where(even, high, low), 8)
-    for ref, at in ((on_ref, on_at), (off_ref, off_at)):
-        ref[0:HALO, :] = object_ref[pl.ds(at, HALO), :]
-        for k in range(FK):
-            ref[(k + 1) * HALO : (k + 2) * HALO, :] = data_ref[pl.ds(at, HALO), k, :]
-
-
-def psf_kernel(coeffs_ref, basis_ref, opening_ref, pr_ref, pl_ref, fl_ref, fr_ref,
-               pupil_ref, field_ref, spec_ref, scale_ref, rows_scr, left_scr):
+    copies = fetch(
+        [
+            (object_hbm.at[pl.ds(off_at, HALO)], off_ref.at[pl.ds(0, HALO)]),
+            (data_hbm.at[pl.ds(off_at, HALO)], off_scr),
+            (object_hbm.at[pl.ds(on_at, HALO)], on_ref.at[pl.ds(0, HALO)]),
+            (data_hbm.at[pl.ds(on_at, HALO)], on_scr),
+        ],
+        sems,
+    )
+    for copy in copies:
+        copy.wait()
+    for k in range(FK):
+        rows = slice((k + 1) * HALO, (k + 2) * HALO)
+        off_ref[rows, :] = off_scr[:, k, :]
+        on_ref[rows, :] = on_scr[:, k, :]
+
+
+def psf_kernel(coeffs_hbm, object_hbm, data_hbm, opening_hbm, basis_hbm, pr_hbm, pl_hbm, fl_hbm, fr_hbm,
+               windows_hbm, rl_hbm, bl_hbm, br_hbm,
+               pupil_ref, field_ref, spec_ref, scale_ref, ext, fl_ref, fr_ref,
+               windows_ref, rl_ref, bl_ref, br_ref,
+               basis_scr, wave_scr, rows_scr, left_scr, coeffs_ref, data_scr, opening_ref, pr_ref, pl_ref, sems):
+    chunks = [(basis_hbm.at[:, pl.ds(j * CHUNK, CHUNK)], basis_scr.at[j]) for j in range(CHUNKS)]
+    copies = fetch(
+        [
+            (coeffs_hbm, coeffs_ref),
+            (object_hbm, ext.at[0, pl.ds(HALO, STRIDE), pl.ds(LANES, 2 * LANES)]),
+            (data_hbm, data_scr),
+        ] + chunks + [
+            (opening_hbm, opening_ref), (pr_hbm, pr_ref), (pl_hbm, pl_ref), (fl_hbm, fl_ref), (fr_hbm, fr_ref),
+            (windows_hbm, windows_ref), (rl_hbm, rl_ref), (bl_hbm, bl_ref), (br_hbm, br_ref),
+        ],
+        sems,
+    )
+    for i in range(1 + FK):
+        ext[i, :, 0:LANES] = jnp.zeros((HEIGHT, LANES), F32)
+        ext[i, :, 3 * LANES :] = jnp.zeros((HEIGHT, LANES), F32)
+        ext[i, STRIDE + 2 * HALO :, LANES : 3 * LANES] = jnp.zeros((HEIGHT - STRIDE - 2 * HALO, 2 * LANES), F32)
+    pupil_ref[...] = jnp.zeros_like(pupil_ref)
+    copies[0].wait()
+    copies[1].wait()
+    copies[2].wait()
+    for k in range(FK):
+        ext[k + 1, HALO : HALO + STRIDE, LANES : 3 * LANES] = data_scr[:, k, :]
+    copies = copies[3:]
     coeffs = jnp.concatenate([coeffs_ref[0, 0], coeffs_ref[1, 0]], axis=0)
     c_high = coeffs.astype(BF16)
     rest = coeffs - c_high.astype(F32)
     c_mid = rest.astype(BF16)
     c_low = (rest - c_mid.astype(F32)).astype(BF16)
-    basis = basis_ref[...]
-    b_high = basis.astype(BF16)
-    b_rest = basis - b_high.astype(F32)
-    b_mid = b_rest.astype(BF16)
-    b_low = (b_rest - b_mid.astype(F32)).astype(BF16)
-    wave = (mm(c_high, b_low) + mm(c_mid, b_mid) + mm(c_low, b_high)) + (mm(c_high, b_mid) + mm(c_mid, b_high)) + mm(c_high, b_high)
+    c_all = jnp.concatenate([c_high, c_mid, c_low], axis=0)
+    for j in range(CHUNKS):
+        copies[j].wait()
+        basis = basis_scr[j]
+        b_high = basis.astype(BF16)
+        b_rest = basis - b_high.astype(F32)
+        b_mid = b_rest.astype(BF16)
+        b_low = (b_rest - b_mid.astype(F32)).astype(BF16)
+        by_high, by_mid, by_low = mm(c_all, b_high), mm(c_all[: 2 * NI], b_mid), mm(c_high, b_low)
+        small = by_low + by_mid[NI:] + by_high[2 * NI :]
+        wave_scr[:, j * CHUNK : (j + 1) * CHUNK] = small + (by_mid[:NI] + by_high[NI : 2 * NI]) + by_high[:NI]
+    wave = wave_scr[...]
     sine, cosine = sin_cos(wave)
+    copies[CHUNKS].wait()
     opening = opening_ref[...]
     re = cosine * opening
     im = sine * opening
-    pupil_ref[...] = jnp.zeros_like(pupil_ref)
     for a in range(PU):
         pupil_ref[a * NI : (a + 1) * NI, 0:PU] = re[:, a * PU : (a + 1) * PU]
         pupil_ref[a * NI : (a + 1) * NI, 64 : 64 + PU] = im[:, a * PU : (a + 1) * PU]
+    copies[CHUNKS + 1].wait()
     mixed = right(pupil_ref[...], pr_ref)
     rows_scr[0] = mixed[:, :LANES]
     rows_scr[1] = mixed[:, LANES:]
@@ -192,6 +243,7 @@
         lanes = slice(n * LANES, (n + 1) * LANES)
         left_scr[0:PU, lanes] = rows_scr[0, pl.ds(n, PU, stride=NI), :]
         left_scr[PU:, lanes] = rows_scr[1, pl.ds(n, PU, stride=NI), :]
+    copies[CHUNKS + 2].wait()
     field = left_wide(pl_ref, left_scr[...])
     field_ref[...] = field
     intensity = field[:PP] * field[:PP] + field[PP:] * field[PP:]
@@ -204,29 +256,29 @@
         [intensity[:, n * LANES : (n + 1) * LANES] * scale[n : n + 1, :] for n in range(NI)], axis=1
     )
     pair = jnp.concatenate([spread[:, : PC * LANES], spread[:, PC * LANES :]], axis=0)
+    copies[CHUNKS + 3].wait()
+    copies[CHUNKS + 4].wait()
     spec_ref[...] = right(to_rows(left(fl_ref, pair)), fr_ref)
-
-
-def misfit_kernel(offsets_ref, kinds_ref, counts_ref, object_ref, data_ref, on_ref, off_ref, spec_ref, windows_ref,
-                  rl_ref, fl_ref, fr_ref, ir_ref, il_ref, gl_ref,
+    for copy in copies[CHUNKS + 5 :]:
+        copy.wait()
+
+
+def misfit_kernel(offsets_ref, kinds_ref, counts_ref, on_ref, off_ref, spec_ref, ext_in, windows_ref, rl_ref, fl_ref, fr_ref,
                   obj_spec_ref, res_spec_ref, centre_ref, on_rim_ref, off_rim_ref, ext, total):
     even = lax.axis_index("patch") % 2 == 0
     on_at = pl.multiple_of(jnp.where(even, STRIDE + HALO, 0), 8)
     off_at = pl.multiple_of(jnp.where(even, 0, STRIDE + HALO), 8)
-    edge = jnp.zeros((HEIGHT, LANES), F32)
     mid = slice(LANES, 3 * LANES)
+    total[...] = jnp.zeros_like(total)
     for i in range(1 + FK):
-        ext[i, :, 0:LANES] = edge
-        ext[i, :, 3 * LANES :] = edge
-        ext[i, STRIDE + 2 * HALO :, mid] = jnp.zeros((HEIGHT - STRIDE - 2 * HALO, 2 * LANES), F32)
-        ext[i, HALO : HALO + STRIDE, mid] = object_ref[...] if i == 0 else data_ref[:, i - 1, :]
+        ext[i] = ext_in[i]
         ext[i, pl.ds(on_at, HALO), mid] = on_ref[i * HALO : (i + 1) * HALO, :]
         ext[i, pl.ds(off_at, HALO), mid] = off_ref[i * HALO : (i + 1) * HALO, :]
 
-    row_base = [pl.multiple_of((offsets_ref[0, c, 0] >> 3) << 3, 8) for c in range(PC)]
-    row_rest = [offsets_ref[0, c, 0] & 7 for c in range(PC)]
+    row_base = [pl.multiple_of((offsets_ref[0, 0, c] >> 3) << 3, 8) for c in range(PC)]
+    row_rest = [offsets_ref[0, 0, c] & 7 for c in range(PC)]
     base = [0, LANES, LANES, 2 * LANES]
-    shift = [LANES + c * STRIDE - HALO - base[c] + offsets_ref[0, c, 1] for c in range(PC)]
+    shift = [LANES + c * STRIDE - HALO - base[c] + offsets_ref[0, 1, c] for c in range(PC)]
 
     def cut(i, c):
         block = ext[i, pl.ds(row_base[c], TALL), base[c] : base[c] + 2 * LANES]
@@ -239,22 +291,21 @@
     obj_spec_ref[...] = obj
     spec = spec_ref[...]
     o_re, o_im, s_re, s_im = obj[:, :LANES], obj[:, LANES:], spec[:, :LANES], spec[:, LANES:]
-    product = jnp.concatenate([o_re * s_re - o_im * s_im, o_re * s_im + o_im * s_re], axis=1)
-    predicted = left(il_ref, to_lanes(right(product, ir_ref)))
+    product = jnp.concatenate([o_re * s_re - o_im * s_im, -(o_re * s_im + o_im * s_re)], axis=1)
+    predicted = left(fl_ref, to_lanes(right(product, fr_ref)))
     parts = []
     for k in range(FK):
         for c in range(PC):
             usable = jnp.where(c < counts_ref[0], 1.0, 0.0).astype(F32)
             lanes = slice(c * LANES, (c + 1) * LANES)
-            here = predicted[k * PP : (k + 1) * PP, lanes] * (1.0 / (PP * PP))
+            here = predicted[k * PP : (k + 1) * PP, lanes] * ((1 - 2 * k) / (PP * PP))
             parts.append((here - windows[c] * cut(k + 1, c)) * usable)
     residual = jnp.concatenate([jnp.concatenate(parts[k * PC : (k + 1) * PC], axis=1) for k in range(FK)], axis=0)
     res = right(to_rows(left(fl_ref, residual)), fr_ref)
     res_spec_ref[...] = res
     r_re, r_im = res[:, :LANES], res[:, LANES:]
-    back = jnp.concatenate([s_re * r_re + s_im * r_im, s_re * r_im - s_im * r_re], axis=1)
-    grad = left(gl_ref, to_lanes(right(back, ir_ref)))
-    total[...] = jnp.zeros_like(total)
+    back = jnp.concatenate([s_re * r_re + s_im * r_im, s_im * r_re - s_re * r_im], axis=1)
+    grad = left_part(fl_ref, to_lanes(right(back, fr_ref)))
     for c in range(PC):
         mine = windows[c] * grad[:, c * LANES : (c + 1) * LANES] * (1.0 / (PP * PP))
         mine = pltpu.roll(jnp.concatenate([mine, jnp.zeros((TALL - PP, LANES), F32)], axis=0), row_rest[c], 0)
@@ -266,12 +317,15 @@
     off_rim_ref[...] = total[pl.ds(off_at, HALO), mid]
 
 
-def mode_kernel(obj_spec_ref, res_spec_ref, field_ref, scale_ref, pupil_ref, basis_ref, ir_ref, il_ref, bl_ref, br_ref,
-                out_ref, rows_scr, flat_scr):
+def spread_grad_kernel(obj_spec_ref, res_spec_ref, fl_ref, fr_ref, grad_ref):
     obj, res = obj_spec_ref[...], res_spec_ref[...]
     o_re, o_im, r_re, r_im = obj[:, :LANES], obj[:, LANES:], res[:, :LANES], res[:, LANES:]
-    back = jnp.concatenate([o_re * r_re + o_im * r_im, o_re * r_im - o_im * r_re], axis=1)
-    grad = left(il_ref, to_lanes(right(back, ir_ref)))
+    back = jnp.concatenate([o_re * r_re + o_im * r_im, o_im * r_re - o_re * r_im], axis=1)
+    grad_ref[...] = left(fl_ref, to_lanes(right(back, fr_ref)))
+
+
+def mode_kernel(grad_ref, field_ref, scale_ref, pupil_ref, bl_ref, br_ref, basis_hbm, out_ref, rows_scr, flat_ref, basis_scr, sems):
+    copies = fetch([(basis_hbm.at[:, pl.ds(j * CHUNK, CHUNK)], basis_scr.at[j]) for j in range(CHUNKS)], sems)
     re_parts, im_parts = [], []
     for n in range(NI):
         k, c = divmod(n, PC)
@@ -279,7 +333,7 @@
         f_re, f_im = field_ref[:PP, lanes], field_ref[PP:, lanes]
         scale = scale_ref[n : n + 1, :]
         spread = (f_re * f_re + f_im * f_im) * scale
-        mine = grad[k * PP : (k + 1) * PP, c * LANES : (c + 1) * LANES] * (1.0 / (PP * PP))
+        mine = grad_ref[k * PP : (k + 1) * PP, c * LANES : (c + 1) * LANES] * ((1 - 2 * k) / (PP * PP))
         mean = jnp.sum(jnp.sum(mine * spread, axis=0, keepdims=True), axis=1, keepdims=True)
         slope = 2.0 * scale * (mine - mean)
         re_parts.append(f_re * slope)
@@ -295,34 +349,57 @@
     crossed = pupil * pltpu.roll(pupil_grad, 64, 1)
     slopes = crossed - pltpu.roll(crossed, 64, 1)
     for a in range(PU):
-        flat_scr[:, a * PU : (a + 1) * PU] = slopes[a * NI : (a + 1) * NI, 0:PU]
-    high, low = split(flat_scr[...])
-    b_high, b_low = split(basis_ref[...])
+        flat_ref[:, a * PU : (a + 1) * PU] = slopes[a * NI : (a + 1) * NI, 0:PU]
+    flat_high, flat_low = split(flat_ref[...])
+    both = jnp.concatenate([flat_high, flat_low], axis=0)
 
     def by_modes(a, b):
         return lax.dot_general(a, b, (((1,), (1,)), ((), ())), preferred_element_type=F32)
 
-    both = by_modes(jnp.concatenate([high, low], axis=0), b_high)
-    out = both[:NI] + both[NI:] + by_modes(high, b_low)
+    out = jnp.zeros((NI, MODES), F32)
+    for j in range(CHUNKS):
+        copies[j].wait()
+        b_high, b_low = split(basis_scr[j])
+        lanes = slice(j * CHUNK, (j + 1) * CHUNK)
+        first = by_modes(both[:, lanes], b_high)
+        out = out + (first[:NI] + first[NI:] + by_modes(flat_high[:, lanes], b_low))
     out_ref[0, 0] = out[:PC]
     out_ref[1, 0] = out[PC:]
 
 
-def call(kernel, out_shapes, scratch=(), smem=0, inputs=0, name=None):
+def call(kernel, out_shapes, scratch=(), smem=0, near=0, far=0, name=None):
     vmem = pl.BlockSpec(memory_space=pltpu.VMEM)
-    return pl.pallas_call(
+    inner = pl.pallas_call(
         kernel,
         out_shape=out_shapes,
-        in_specs=[pl.BlockSpec(memory_space=pltpu.SMEM)] * smem + [vmem] * inputs,
+        in_specs=[pl.BlockSpec(memory_space=pltpu.SMEM)] * smem + [vmem] * near + [pl.BlockSpec(memory_space=pltpu.HBM)] * far,
         out_specs=jax.tree.map(lambda _: vmem, out_shapes),
         scratch_shapes=list(scratch),
         compiler_params=pltpu.CompilerParams(vmem_limit_bytes=VMEM_LIMIT),
         name=name,
     )
 
+    def run(*operands):
+        placed = list(operands)
+        for i in range(smem + near, smem + near + far):
+            placed[i] = pltpu.with_memory_space_constraint(placed[i], pltpu.HBM)
+        for i in range(smem, smem + near):
+            placed[i] = pltpu.with_memory_space_constraint(placed[i], pltpu.VMEM)
+        return inner(*placed)
+
+    return run
+
 
 def shape(*dims):
-    return jax.ShapeDtypeStruct(dims, F32)
+    return pltpu.VMEM(dims, F32)
+
+
+def sems(count):
+    return pltpu.SemaphoreType.DMA((count,))
+
+
+def like(value):
+    return pltpu.VMEM(value.shape, BF16 if value.dtype == ml_dtypes.bfloat16 else F32)
 
 
 def swap_on(values):
@@ -343,46 +420,63 @@
 
 def body(object_band, data_band, coeffs, mode_basis, offsets, window_ids, counts):
     columns = object_band.shape[1]
-    const = {name: jnp.asarray(value) for name, value in constants().items()}
-    on_send, off_send = call(pack_kernel, [shape(3 * HALO, columns)] * 2, inputs=2, name="pack")(object_band, data_band)
+    host = constants()
+    const = {name: jnp.asarray(value) for name, value in host.items()}
+    room = {name: like(value) for name, value in host.items()}
+    halo_room = pltpu.VMEM((HALO, FK, columns), F32)
+    on_send, off_send = call(
+        pack_kernel, [shape(3 * HALO, columns)] * 2, scratch=[halo_room, halo_room, sems(4)], far=2, name="pack",
+    )(object_band, data_band)
     off_halo = swap_off(off_send)
     on_halo = swap_on(on_send)
-    pupil, field, spec, scale = call(
+    given = ("opening", "pupil_right", "pupil_left", "fwd_left", "fwd_right", "windows", "real_left", "back_left", "back_right")
+    kept = ("fwd_left", "fwd_right", "windows", "real_left", "back_left", "back_right")
+    pupil, field, spec, scale, ext, *kept_values = call(
         psf_kernel,
-        [shape(PU * NI, LANES), shape(2 * PP, NI * LANES), shape(PC * PP, 2 * LANES), shape(NI, LANES)],
-        scratch=[pltpu.VMEM((2, PU * NI, LANES), F32), pltpu.VMEM((2 * PU, NI * LANES), F32)],
-        inputs=7,
+        [shape(PU * NI, LANES), shape(2 * PP, NI * LANES), shape(PC * PP, 2 * LANES), shape(NI, LANES),
+         shape(1 + FK, HEIGHT, 4 * LANES)] + [room[name] for name in kept],
+        scratch=[
+            pltpu.VMEM((CHUNKS, MODES, CHUNK), F32), pltpu.VMEM((NI, PU * PU), F32), pltpu.VMEM((2, PU * NI, LANES), F32),
+            pltpu.VMEM((2 * PU, NI * LANES), F32), pltpu.VMEM((FK, 1, PC, MODES), F32), pltpu.VMEM((STRIDE, FK, columns), F32),
+            room["opening"], room["pupil_right"], room["pupil_left"], sems(CHUNKS + 12),
+        ],
+        far=13,
         name="psf",
-    )(coeffs, mode_basis, const["opening"], const["pupil_right"], const["pupil_left"], const["fwd_left"], const["fwd_right"])
+    )(coeffs, object_band, data_band, const["opening"], mode_basis, *[const[name] for name in given[1:]])
+    here = dict(zip(kept, kept_values))
     obj_spec, res_spec, centre, on_rim, off_rim = call(
         misfit_kernel,
         [shape(PC * PP, 2 * LANES)] * 2 + [shape(STRIDE, columns), shape(HALO, columns), shape(HALO, columns)],
         scratch=[pltpu.VMEM((1 + FK, HEIGHT, 4 * LANES), F32), pltpu.VMEM((HEIGHT, 4 * LANES), F32)],
         smem=3,
-        inputs=12,
+        near=8,
         name="misfit",
     )(
-        offsets, window_ids, counts, object_band, data_band, on_halo, off_halo, spec, const["windows"],
-        const["real_left"], const["fwd_left"], const["fwd_right"], const["inv_right"], const["inv_left"], const["part_left"],
+        jnp.transpose(offsets, (0, 2, 1)), window_ids, counts, on_halo, off_halo, spec, ext,
+        here["windows"], here["real_left"], here["fwd_left"], here["fwd_right"],
     )
     on_rim = swap_on(on_rim)
     off_rim = swap_off(off_rim)
+    spread_grad = call(spread_grad_kernel, shape(2 * PP, PC * LANES), near=4, name="spread_grad")(
+        obj_spec, res_spec, here["fwd_left"], here["fwd_right"]
+    )
     even = lax.axis_index("patch") % 2 == 0
     upper = jnp.where(even, off_rim, on_rim)
     lower = jnp.where(even, on_rim, off_rim)
     rows = jnp.concatenate([centre[:HALO] + upper, centre[HALO : STRIDE - HALO], centre[STRIDE - HALO :] + lower], axis=0)
-    for bit in (4, 1, 2):
-        rows = rows + swap_frames(rows, bit)
+    rows, spread_grad = lax.optimization_barrier((rows, spread_grad))
+    moved = swap_frames(rows, 4)
     coeff_grad = call(
-        mode_kernel,
-        shape(FK, 1, PC, MODES),
-        scratch=[pltpu.VMEM((2, PU * NI, LANES), F32), pltpu.VMEM((NI, PU * PU), F32)],
-        inputs=10,
-        name="modes",
-    )(
-        obj_spec, res_spec, field, scale, pupil, mode_basis,
-        const["inv_right"], const["inv_left"], const["back_left"], const["back_right"],
-    )
+        mode_kernel, jax.ShapeDtypeStruct((FK, 1, PC, MODES), F32),
+        scratch=[
+            pltpu.VMEM((2, PU * NI, LANES), F32), pltpu.VMEM((NI, PU * PU), F32), pltpu.VMEM((CHUNKS, MODES, CHUNK), F32), sems(CHUNKS),
+        ],
+        near=6, far=1, name="modes",
+    )(spread_grad, field, scale, pupil, here["back_left"], here["back_right"], mode_basis)
+    rows = rows + moved
+    rows, coeff_grad = lax.optimization_barrier((rows, coeff_grad))
+    rows = rows + swap_frames(rows, 1)
+    rows = rows + swap_frames(rows, 2)
     return rows, coeff_grad
 
 

time: 51.4 us -> 42.9 us (0.83)
  Pallas kernels: 17.4 us -> 13.1 us
  waiting for transfers between devices: 10.9 us -> 7.71 us
  local copies, waits for them, and re-layouts: 2.7 us -> 0.01 us
  starting transfers between devices: 17.3 us -> 19.6 us
  other arithmetic: 1.43 us -> 0.68 us
    pallas_call x4 -> x5, Pallas kernels: 17.4 us -> 13.1 us  [run(): return inner(*placed)]
    ppermute x2, waiting for transfers between devices: 5.02 us -> 2.69 us  [swap_off(): return lax.ppermute(values, 'patch', pairs + [(j, i) for i, j in pairs])]
    ppermute x2, starting transfers between devices: 11.1 us -> 13.1 us  [swap_off(): return lax.ppermute(values, 'patch', pairs + [(j, i) for i, j in pairs])]
    unnamed x5 -> x4, local copies, waits for them, and re-layouts: 1.97 us -> 0.01 us
    ppermute x3, waiting for transfers between devices: 5.83 us -> 5.01 us  [swap_frames(): return lax.ppermute(values, 'frames', [(i, i ^ bit) for i in range(count)])]
    add x1, other arithmetic: 0.77 us -> 0.01 us  [body(): centre[:HALO] + upper]
    slice x1, local copies, waits for them, and re-layouts: 0.72 us -> 0.01 us  [body(): centre[HALO:STRIDE - HALO]]
  transfers between devices with their start and end apart: 7 -> 7, of which waited for: 3 -> 3; matrix products, arithmetic and copies ran while one was open for 4% -> 0% of each run, Pallas kernels for 21% -> 21%
where the time goes in v1:
time: 42.9 us; the launch traced here: 42.5 us
  starting transfers between devices  19.6 us (46%)
  Pallas kernels  13.1 us (31%)
  waiting for transfers between devices  7.71 us (18%)
  between operations  1.45 us (3%)
  other arithmetic  0.68 us (2%)
    ppermute x2, starting transfers between devices, swap_off(): return lax.ppermute(values, 'patch', pairs + [(j, i) for i, j in pairs])  13.1 us
    pallas_call x5, Pallas kernels, run(): return inner(*placed)  13.1 us
    ppermute x3, starting transfers between devices, swap_frames(): return lax.ppermute(values, 'frames', [(i, i ^ bit) for i in range(count)])  6.33 us
    ppermute x3, waiting for transfers between devices, swap_frames(): return lax.ppermute(values, 'frames', [(i, i ^ bit) for i in range(count)])  5.01 us
    ppermute x2, waiting for transfers between devices, swap_off(): return lax.ppermute(values, 'patch', pairs + [(j, i) for i, j in pairs])  2.69 us
  transfers between devices with their start and end apart: 7, of which 3 were waited for; matrix products, arithmetic and copies ran while one was open for 0% of the time, Pallas kernels for 21%

profile of v1, /device:TPU:6, one launch (start us, length us, event | category | flops | bytes accessed | tf_op | source)
XLA Modules:
  0.0 42.5 jit_solution(12153068940864656628)
XLA Ops:
  0.6 0.0 copy-start
  0.6 0.0 copy-start.1
  0.6 0.9 %pack.1 = (f32[72,256]{1,0:T(8,128)S(1)}, f32[72,256]{1,0:T(8,128)S(1)}) custom-call(f32[64,256]{1,0:T(8,128)} %object_hbm.3, f32[64,2,256]{2,1,0:T(2,128)} %data_hbm.3), custom_call_target="tpu_custom_call" | custom-call | tf_op jit(solution)/shard_map/pack/pallas_call | solution.py:388
  1.6 0.1 collective-permute-start
  1.7 8.6 %collective-permute-start.1 = (f32[72,256]{1,0:T(8,128)S(1)}, f32[72,256]{1,0:T(8,128)S(1)}, u32[]{:S(2)}, u32[]{:S(2)}) collective-permute-start(f32[72,256]{1,0:T(8,128)S(1)} %get-tuple-element.25), channel_id=1, source_target_pairs={{1,2},{3,4},{5,6},{7,8},{9,10},{11,12},{13,14},{15,16},{17,18},{19... | collective-permute-start | bytes 221192 | tf_op jit(solution)/shard_map/ppermute | solution.py:413
  10.9 4.3 %psf.1 = (f32[384,128]{1,0:T(8,128)S(1)}, f32[192,1024]{1,0:T(8,128)S(1)}, f32[384,256]{1,0:T(8,128)S(1)}, f32[8,128]{1,0:T(8,128)S(1)}, f32[3,120,512]{2,1,0:T(...) custom-call(f32[2,1,4,200]{3,2,1,0:T(4,128)} %coeffs_hbm.1, ...), custom_call_target="tpu_custom_call" | custom-call | tf_op jit(solution)/shard_map/psf/pallas_call | solution.py:388
  15.2 0.0 collective-permute-done.on_ref
  15.2 0.0 collective-permute-done.1.off_ref
  15.2 0.0 copy-done
  15.2 0.0 copy-done.1
  15.2 3.4 %misfit.1 = (f32[384,256]{1,0:T(8,128)S(1)}, f32[384,256]{1,0:T(8,128)S(1)}, f32[64,256]{1,0:T(8,128)S(1)}, f32[24,256]{1,0:T(8,128)S(1)}, f32[24,256]{1,0:T(8,128)S(1)}) custom-call(s32[1,2,4]{2,1,0:T(2,128)S(1)} %bitcast.1, s32[1,4]{1,0:T(1,128)S(1)} %copy-done.1, s32[1]{0:T(128)S(6)} %copy.18.counts_ref, f32[72,256]{1,0:T(8,128)S(1)} %collective-permute-done.on_ref, ...), custom_call_target="tpu_custom_call" | custom-call | tf_op jit(solution)/shard_map/misfit/pallas_call | solution.py:388
  18.6 4.5 %collective-permute-start.2 = (f32[24,256]{1,0:T(8,128)S(1)}, f32[24,256]{1,0:T(8,128)S(1)}, u32[]{:S(2)}, u32[]{:S(2)}) collective-permute-start(f32[24,256]{1,0:T(8,128)S(1)} %get-tuple-element.33), channel_id=1, source_target_pairs={{1,2},{3,4},{5,6},{7,8},{9,10},{11,12},{13,14},{15,16},{17,18},{19... | collective-permute-start | bytes 73736 | tf_op jit(solution)/shard_map/ppermute | solution.py:413
  23.1 0.1 collective-permute-start.3
  23.2 0.8 %spread_grad.1.grad_ref = f32[192,512]{1,0:T(8,128)S(1)} custom-call(f32[384,256]{1,0:T(8,128)S(1)} %get-tuple-element.35.obj_spec_ref, f32[384,256]{1,0:T(8,128)S(1)} %get-tuple-element.36.res_spec_ref, bf16[384,192]{1,0:T(8,128)(2,1)S(1)} %get-tuple-element.30.fl_ref, bf16[512,256]{1,0:T(8,128)(2,1)S(1)} %get-tuple-element.31.fr_ref), custom_call_target="tpu_custom_call" | custom-call | tf_op jit(solution)/shard_map/spread_grad/pallas_call | solution.py:388
  24.1 2.7 %collective-permute-done.2 = f32[24,256]{1,0:T(8,128)S(1)} collective-permute-done((f32[24,256]{1,0:T(8,128)S(1)}, f32[24,256]{1,0:T(8,128)S(1)}, u32[]{:S(2)}, u32[]{:S(2)}) %collective-permute-start.2) | collective-permute-done | bytes 24608 | tf_op jit(solution)/shard_map/ppermute | solution.py:413
  26.8 0.0 collective-permute-done.3
  26.8 1.1 %collective-permute-start.4 = (f32[64,256]{1,0:T(8,128)S(1)}, f32[64,256]{1,0:T(8,128)S(1)}, u32[]{:S(2)}, u32[]{:S(2)}) collective-permute-start(f32[64,256]{1,0:T(8,128)S(1)} %pad_maximum_fusion), channel_id=1, source_target_pairs={{0,128},{32,160},{64,192},{96,224},{128,0},{160,32},{192,64},{224,... | collective-permute-start | bytes 196616 | tf_op jit(solution)/shard_map/ppermute | solution.py:418
  27.9 3.7 %modes.1 = f32[2,1,4,200]{3,2,1,0:T(4,128)} custom-call(f32[192,512]{1,0:T(8,128)S(1)} %spread_grad.1.grad_ref, f32[192,1024]{1,0:T(8,128)S(1)} %get-tuple-element.39.field_ref, f32[8,128]{1,0:T(8,128)S(1)} %get-tuple-element.40.scale_ref, f32[384,128]{1,0:T(8,128)S(1)} %get-tuple-element.41.pupil_ref, bf16[192,192]{1,0:T(8,128)(2,1)S(1)} %get-tuple-element.42.bl_ref, ...), custom_call_target="tpu_custom_call" | custom-call | tf_op jit(solution)/shard_map/modes/pallas_call | solution.py:388
  31.6 0.0 collective-permute-done.4
  31.6 1.7 %collective-permute-start.5 = (f32[64,256]{1,0:T(8,128)S(1)}, f32[64,256]{1,0:T(8,128)S(1)}, u32[]{:S(2)}, u32[]{:S(2)}) collective-permute-start(f32[64,256]{1,0:T(8,128)S(1)} %add.22), channel_id=1, source_target_pairs={{0,32},{32,0},{64,96},{96,64},{128,160},{160,128},{192,224},{224,1... | collective-permute-start | bytes 196616 | tf_op jit(solution)/shard_map/ppermute | solution.py:418
  33.3 2.7 %collective-permute-done.5 = f32[64,256]{1,0:T(8,128)S(1)} collective-permute-done((f32[64,256]{1,0:T(8,128)S(1)}, f32[64,256]{1,0:T(8,128)S(1)}, u32[]{:S(2)}, u32[]{:S(2)}) %collective-permute-start.5) | collective-permute-done | bytes 65568 | tf_op jit(solution)/shard_map/ppermute | solution.py:418
  36.0 3.5 %collective-permute-start.6 = (f32[64,256]{1,0:T(8,128)S(1)}, f32[64,256]{1,0:T(8,128)S(1)}, u32[]{:S(2)}, u32[]{:S(2)}) collective-permute-start(f32[64,256]{1,0:T(8,128)S(1)} %add.23), channel_id=1, source_target_pairs={{0,64},{32,96},{64,0},{96,32},{128,192},{160,224},{192,128},{224,1... | collective-permute-start | bytes 196616 | tf_op jit(solution)/shard_map/ppermute | solution.py:418
  39.5 2.3 %collective-permute-done.6 = f32[64,256]{1,0:T(8,128)S(1)} collective-permute-done((f32[64,256]{1,0:T(8,128)S(1)}, f32[64,256]{1,0:T(8,128)S(1)}, u32[]{:S(2)}, u32[]{:S(2)}) %collective-permute-start.6) | collective-permute-done | bytes 65568 | tf_op jit(solution)/shard_map/ppermute | solution.py:418
  41.8 0.6 %add.24 = f32[64,256]{1,0:T(8,128)} add(f32[64,256]{1,0:T(8,128)S(1)} %add.23, f32[64,256]{1,0:T(8,128)S(1)} %collective-permute-done.6) | non-fusion elementwise | flops 16384 | bytes 196608 | tf_op jit(solution)/shard_map/add | solution.py:479
  (5 shorter events, 0.0 us)
Async XLA Ops:
  0.6 14.6 %copy-start = (s32[1,4,2]{1,2,0:T(2,128)S(1)}, s32[1,4,2]{1,2,0:T(2,128)}, u32[]{:S(2)}) copy-start(s32[1,4,2]{1,2,0:T(2,128)} %param.20) | copy-start | bytes 100
  0.6 14.6 %copy-start.1 = (s32[1,4]{1,0:T(1,128)S(1)}, s32[1,4]{1,0:T(1,128)}, u32[]{:S(2)}) copy-start(s32[1,4]{1,0:T(1,128)} %kinds_ref.1) | copy-start | bytes 52
  1.6 13.6 %collective-permute-start = (f32[72,256]{1,0:T(8,128)S(1)}, f32[72,256]{1,0:T(8,128)S(1)}, u32[]{:S(2)}, u32[]{:S(2)}) collective-permute-start(f32[72,256]{1,0:T(8,128)S(1)} %get-tuple-element.24), channel_id=1, source_target_pairs={{0,1},{1,0},{2,3},{3,2},{4,5},{5,4},{6,7},{7,6},{8,9},{9,8},{10,11... | collective-permute-start | bytes 221192 | tf_op jit(solution)/shard_map/ppermute | solution.py:407
  1.7 13.5 %collective-permute-start.1 = (f32[72,256]{1,0:T(8,128)S(1)}, f32[72,256]{1,0:T(8,128)S(1)}, u32[]{:S(2)}, u32[]{:S(2)}) collective-permute-start(f32[72,256]{1,0:T(8,128)S(1)} %get-tuple-element.25), channel_id=1, source_target_pairs={{1,2},{3,4},{5,6},{7,8},{9,10},{11,12},{13,14},{15,16},{17,18},{19... | collective-permute-start | bytes 221192 | tf_op jit(solution)/shard_map/ppermute | solution.py:413
  18.6 8.2 %collective-permute-start.2 = (f32[24,256]{1,0:T(8,128)S(1)}, f32[24,256]{1,0:T(8,128)S(1)}, u32[]{:S(2)}, u32[]{:S(2)}) collective-permute-start(f32[24,256]{1,0:T(8,128)S(1)} %get-tuple-element.33), channel_id=1, source_target_pairs={{1,2},{3,4},{5,6},{7,8},{9,10},{11,12},{13,14},{15,16},{17,18},{19... | collective-permute-start | bytes 73736 | tf_op jit(solution)/shard_map/ppermute | solution.py:413
  23.1 3.7 %collective-permute-start.3 = (f32[24,256]{1,0:T(8,128)S(1)}, f32[24,256]{1,0:T(8,128)S(1)}, u32[]{:S(2)}, u32[]{:S(2)}) collective-permute-start(f32[24,256]{1,0:T(8,128)S(1)} %get-tuple-element.34), channel_id=1, source_target_pairs={{0,1},{1,0},{2,3},{3,2},{4,5},{5,4},{6,7},{7,6},{8,9},{9,8},{10,11... | collective-permute-start | bytes 73736 | tf_op jit(solution)/shard_map/ppermute | solution.py:407
  26.8 4.8 %collective-permute-start.4 = (f32[64,256]{1,0:T(8,128)S(1)}, f32[64,256]{1,0:T(8,128)S(1)}, u32[]{:S(2)}, u32[]{:S(2)}) collective-permute-start(f32[64,256]{1,0:T(8,128)S(1)} %pad_maximum_fusion), channel_id=1, source_target_pairs={{0,128},{32,160},{64,192},{96,224},{128,0},{160,32},{192,64},{224,... | collective-permute-start | bytes 196616 | tf_op jit(solution)/shard_map/ppermute | solution.py:418
  31.6 4.4 %collective-permute-start.5 = (f32[64,256]{1,0:T(8,128)S(1)}, f32[64,256]{1,0:T(8,128)S(1)}, u32[]{:S(2)}, u32[]{:S(2)}) collective-permute-start(f32[64,256]{1,0:T(8,128)S(1)} %add.22), channel_id=1, source_target_pairs={{0,32},{32,0},{64,96},{96,64},{128,160},{160,128},{192,224},{224,1... | collective-permute-start | bytes 196616 | tf_op jit(solution)/shard_map/ppermute | solution.py:418
  36.0 5.9 %collective-permute-start.6 = (f32[64,256]{1,0:T(8,128)S(1)}, f32[64,256]{1,0:T(8,128)S(1)}, u32[]{:S(2)}, u32[]{:S(2)}) collective-permute-start(f32[64,256]{1,0:T(8,128)S(1)} %add.23), channel_id=1, source_target_pairs={{0,64},{32,96},{64,0},{96,32},{128,192},{160,224},{192,128},{224,1... | collective-permute-start | bytes 196616 | tf_op jit(solution)/shard_map/ppermute | solution.py:418

commit v2 on v1

--- a/solution.py
+++ b/solution.py
@@ -22,7 +22,7 @@
 HEIGHT = STRIDE + 2 * HALO + 8
 F32 = jnp.float32
 BF16 = jnp.bfloat16
-VMEM_LIMIT = 8 * 1024 * 1024
+VMEM_LIMIT = 16 * 1024 * 1024
 CHUNK = 768
 CHUNKS = PU * PU // CHUNK
 
@@ -56,12 +56,13 @@
     fwd_left = np.block([[full_re, -full_im], [full_im, full_re]])
     real_left = np.concatenate([full_re, full_im], axis=0)
 
-    def stack(matrix):
-        return np.concatenate(halves(matrix), axis=0)
-
-    def twice(matrix):
+    def tall(matrix):
         high, low = halves(matrix)
-        return np.concatenate([high, low], axis=1)
+        return np.concatenate([high, low, high], axis=0)
+
+    def wide(matrix):
+        high, low = halves(matrix)
+        return np.concatenate([high, low, high], axis=1)
 
     side = np.arange(PP) + 0.5
     windows = np.zeros((4, PP, LANES), np.float32)
@@ -73,13 +74,13 @@
     centre = np.arange(PU) + 0.5 - 0.5 * PU
     opening = (centre[:, None] ** 2 + centre[None, :] ** 2 <= (0.5 * PU) ** 2).reshape(1, PU * PU)
     return {
-        "fwd_right": stack(fwd_right),
-        "pupil_right": stack(pupil_right),
-        "pupil_left": twice(pupil_left),
-        "fwd_left": stack(fwd_left),
-        "real_left": twice(real_left),
-        "back_left": stack(pupil_left.T.copy()),
-        "back_right": stack(pupil_right.T.copy()),
+        "fwd_right": tall(fwd_right),
+        "pupil_right": tall(pupil_right),
+        "pupil_left": wide(pupil_left),
+        "fwd_left": wide(fwd_left),
+        "real_left": wide(real_left),
+        "back_left": wide(pupil_left.T),
+        "back_right": tall(pupil_right.T),
         "windows": windows,
         "opening": opening.astype(np.float32),
     }
@@ -94,32 +95,14 @@
     return jnp.dot(a, b, preferred_element_type=F32)
 
 
-def right(values, matrix_ref):
-    depth = matrix_ref.shape[0] // 2
-    rows = values.shape[0]
+def right(values, matrix):
     high, low = split(values)
-    both = mm(jnp.concatenate([high, low], axis=0), matrix_ref[:depth])
-    return both[:rows] + both[rows:] + mm(high, matrix_ref[depth:])
-
-
-def left(matrix_ref, values):
-    rows = matrix_ref.shape[0] // 2
+    return mm(jnp.concatenate([high, high, low], axis=1), matrix[...])
+
+
+def left(matrix, values):
     high, low = split(values)
-    both = mm(matrix_ref[...], high)
-    return both[:rows] + both[rows:] + mm(matrix_ref[:rows], low)
-
-
-def left_part(matrix_ref, values):
-    rows = matrix_ref.shape[0] // 2
-    half = rows // 2
-    high, low = split(values)
-    return mm(matrix_ref[:half], high) + mm(matrix_ref[rows : rows + half], high) + mm(matrix_ref[:half], low)
-
-
-def left_wide(matrix_ref, values):
-    depth = values.shape[0]
-    high, low = split(values)
-    return mm(matrix_ref[...], jnp.concatenate([high, high], axis=0)) + mm(matrix_ref[:, :depth], low)
+    return mm(matrix[...], jnp.concatenate([high, high, low], axis=0))
 
 
 def to_rows(spectrum):
@@ -160,7 +143,47 @@
     return copies
 
 
-def pack_kernel(object_hbm, data_hbm, on_ref, off_ref, on_scr, off_scr, sems):
+def is_early():
+    return lax.axis_index("patch") % 8 == 0
+
+
+def pupil_part(coeffs_hbm, opening_hbm, basis_hbm, pupil_ref, basis_scr, wave_scr, coeffs_ref, opening_ref, sems):
+    copies = fetch(
+        [(coeffs_hbm, coeffs_ref)]
+        + [(basis_hbm.at[:, pl.ds(j * CHUNK, CHUNK)], basis_scr.at[j]) for j in range(CHUNKS)]
+        + [(opening_hbm, opening_ref)],
+        sems,
+    )
+    pupil_ref[...] = jnp.zeros_like(pupil_ref)
+    copies[0].wait()
+    coeffs = jnp.concatenate([coeffs_ref[0, 0], coeffs_ref[1, 0]], axis=0)
+    c_high = coeffs.astype(BF16)
+    rest = coeffs - c_high.astype(F32)
+    c_mid = rest.astype(BF16)
+    c_low = (rest - c_mid.astype(F32)).astype(BF16)
+    c_all = jnp.concatenate([c_high, c_mid, c_low], axis=0)
+    for j in range(CHUNKS):
+        copies[1 + j].wait()
+        basis = basis_scr[j]
+        b_high = basis.astype(BF16)
+        b_rest = basis - b_high.astype(F32)
+        b_mid = b_rest.astype(BF16)
+        b_low = (b_rest - b_mid.astype(F32)).astype(BF16)
+        by_high, by_mid, by_low = mm(c_all, b_high), mm(c_all[: 2 * NI], b_mid), mm(c_high, b_low)
+        small = by_low + by_mid[NI:] + by_high[2 * NI :]
+        wave_scr[:, j * CHUNK : (j + 1) * CHUNK] = small + (by_mid[:NI] + by_high[NI : 2 * NI]) + by_high[:NI]
+    copies[1 + CHUNKS].wait()
+    sine, cosine = sin_cos(wave_scr[...])
+    opening = opening_ref[...]
+    re = cosine * opening
+    im = sine * opening
+    for a in range(PU):
+        pupil_ref[a * NI : (a + 1) * NI, 0:PU] = re[:, a * PU : (a + 1) * PU]
+        pupil_ref[a * NI : (a + 1) * NI, 64 : 64 + PU] = im[:, a * PU : (a + 1) * PU]
+
+
+def pack_kernel(object_hbm, data_hbm, coeffs_hbm, opening_hbm, basis_hbm, pr_hbm, pl_hbm, fl_hbm, fr_hbm,
+                on_ref, off_ref, pupil_ref, pr_ref, pl_ref, fl_ref, fr_ref, on_scr, off_scr, send_sems, matrix_sems, *scratch):
     even = lax.axis_index("patch") % 2 == 0
     low, high = STRIDE - HALO, 0
     on_at = pl.multiple_of(jnp.where(even, low, high), 8)
@@ -172,8 +195,16 @@
             (object_hbm.at[pl.ds(on_at, HALO)], on_ref.at[pl.ds(0, HALO)]),
             (data_hbm.at[pl.ds(on_at, HALO)], on_scr),
         ],
-        sems,
-    )
+        send_sems,
+    )
+
+    @pl.when(is_early())
+    def _():
+        matrices = fetch([(pr_hbm, pr_ref), (pl_hbm, pl_ref), (fl_hbm, fl_ref), (fr_hbm, fr_ref)], matrix_sems)
+        pupil_part(coeffs_hbm, opening_hbm, basis_hbm, pupil_ref, *scratch)
+        for copy in matrices:
+            copy.wait()
+
     for copy in copies:
         copy.wait()
     for k in range(FK):
@@ -182,20 +213,14 @@
         on_ref[rows, :] = on_scr[:, k, :]
 
 
-def psf_kernel(coeffs_hbm, object_hbm, data_hbm, opening_hbm, basis_hbm, pr_hbm, pl_hbm, fl_hbm, fr_hbm,
+def psf_kernel(pupil_in, pr_in, pl_in, fl_in, fr_in, coeffs_hbm, opening_hbm, basis_hbm, object_hbm, data_hbm, pr_hbm, pl_hbm, fl_hbm, fr_hbm,
                windows_hbm, rl_hbm, bl_hbm, br_hbm,
-               pupil_ref, field_ref, spec_ref, scale_ref, ext, fl_ref, fr_ref,
-               windows_ref, rl_ref, bl_ref, br_ref,
-               basis_scr, wave_scr, rows_scr, left_scr, coeffs_ref, data_scr, opening_ref, pr_ref, pl_ref, sems):
-    chunks = [(basis_hbm.at[:, pl.ds(j * CHUNK, CHUNK)], basis_scr.at[j]) for j in range(CHUNKS)]
+               pupil_ref, pr_ref, pl_ref, fl_ref, fr_ref, field_ref, spec_ref, scale_ref, ext, windows_ref, rl_ref, bl_ref, br_ref,
+               rows_scr, left_scr, data_scr, sems, matrix_sems, *scratch):
     copies = fetch(
         [
-            (coeffs_hbm, coeffs_ref),
             (object_hbm, ext.at[0, pl.ds(HALO, STRIDE), pl.ds(LANES, 2 * LANES)]),
-            (data_hbm, data_scr),
-        ] + chunks + [
-            (opening_hbm, opening_ref), (pr_hbm, pr_ref), (pl_hbm, pl_ref), (fl_hbm, fl_ref), (fr_hbm, fr_ref),
-            (windows_hbm, windows_ref), (rl_hbm, rl_ref), (bl_hbm, bl_ref), (br_hbm, br_ref),
+            (data_hbm, data_scr), (windows_hbm, windows_ref), (rl_hbm, rl_ref), (bl_hbm, bl_ref), (br_hbm, br_ref),
         ],
         sems,
     )
@@ -203,39 +228,13 @@
         ext[i, :, 0:LANES] = jnp.zeros((HEIGHT, LANES), F32)
         ext[i, :, 3 * LANES :] = jnp.zeros((HEIGHT, LANES), F32)
         ext[i, STRIDE + 2 * HALO :, LANES : 3 * LANES] = jnp.zeros((HEIGHT - STRIDE - 2 * HALO, 2 * LANES), F32)
-    pupil_ref[...] = jnp.zeros_like(pupil_ref)
-    copies[0].wait()
-    copies[1].wait()
-    copies[2].wait()
-    for k in range(FK):
-        ext[k + 1, HALO : HALO + STRIDE, LANES : 3 * LANES] = data_scr[:, k, :]
-    copies = copies[3:]
-    coeffs = jnp.concatenate([coeffs_ref[0, 0], coeffs_ref[1, 0]], axis=0)
-    c_high = coeffs.astype(BF16)
-    rest = coeffs - c_high.astype(F32)
-    c_mid = rest.astype(BF16)
-    c_low = (rest - c_mid.astype(F32)).astype(BF16)
-    c_all = jnp.concatenate([c_high, c_mid, c_low], axis=0)
-    for j in range(CHUNKS):
-        copies[j].wait()
-        basis = basis_scr[j]
-        b_high = basis.astype(BF16)
-        b_rest = basis - b_high.astype(F32)
-        b_mid = b_rest.astype(BF16)
-        b_low = (b_rest - b_mid.astype(F32)).astype(BF16)
-        by_high, by_mid, by_low = mm(c_all, b_high), mm(c_all[: 2 * NI], b_mid), mm(c_high, b_low)
-        small = by_low + by_mid[NI:] + by_high[2 * NI :]
-        wave_scr[:, j * CHUNK : (j + 1) * CHUNK] = small + (by_mid[:NI] + by_high[NI : 2 * NI]) + by_high[:NI]
-    wave = wave_scr[...]
-    sine, cosine = sin_cos(wave)
-    copies[CHUNKS].wait()
-    opening = opening_ref[...]
-    re = cosine * opening
-    im = sine * opening
-    for a in range(PU):
-        pupil_ref[a * NI : (a + 1) * NI, 0:PU] = re[:, a * PU : (a + 1) * PU]
-        pupil_ref[a * NI : (a + 1) * NI, 64 : 64 + PU] = im[:, a * PU : (a + 1) * PU]
-    copies[CHUNKS + 1].wait()
+    @pl.when(jnp.logical_not(is_early()))
+    def _():
+        matrices = fetch([(pr_hbm, pr_ref), (pl_hbm, pl_ref), (fl_hbm, fl_ref), (fr_hbm, fr_ref)], matrix_sems)
+        pupil_part(coeffs_hbm, opening_hbm, basis_hbm, pupil_ref, *scratch)
+        for copy in matrices:
+            copy.wait()
+
     mixed = right(pupil_ref[...], pr_ref)
     rows_scr[0] = mixed[:, :LANES]
     rows_scr[1] = mixed[:, LANES:]
@@ -243,8 +242,7 @@
         lanes = slice(n * LANES, (n + 1) * LANES)
         left_scr[0:PU, lanes] = rows_scr[0, pl.ds(n, PU, stride=NI), :]
         left_scr[PU:, lanes] = rows_scr[1, pl.ds(n, PU, stride=NI), :]
-    copies[CHUNKS + 2].wait()
-    field = left_wide(pl_ref, left_scr[...])
+    field = left(pl_ref, left_scr[...])
     field_ref[...] = field
     intensity = field[:PP] * field[:PP] + field[PP:] * field[PP:]
     sums = jnp.concatenate(
@@ -256,11 +254,11 @@
         [intensity[:, n * LANES : (n + 1) * LANES] * scale[n : n + 1, :] for n in range(NI)], axis=1
     )
     pair = jnp.concatenate([spread[:, : PC * LANES], spread[:, PC * LANES :]], axis=0)
-    copies[CHUNKS + 3].wait()
-    copies[CHUNKS + 4].wait()
     spec_ref[...] = right(to_rows(left(fl_ref, pair)), fr_ref)
-    for copy in copies[CHUNKS + 5 :]:
+    for copy in copies:
         copy.wait()
+    for k in range(FK):
+        ext[k + 1, HALO : HALO + STRIDE, LANES : 3 * LANES] = data_scr[:, k, :]
 
 
 def misfit_kernel(offsets_ref, kinds_ref, counts_ref, on_ref, off_ref, spec_ref, ext_in, windows_ref, rl_ref, fl_ref, fr_ref,
@@ -287,25 +285,20 @@
 
     windows = [windows_ref[kinds_ref[0, c]] for c in range(PC)]
     weighted = jnp.concatenate([windows[c] * cut(0, c) for c in range(PC)], axis=1)
-    obj = right(to_rows(left_wide(rl_ref, weighted)), fr_ref)
+    obj = right(to_rows(left(rl_ref, weighted)), fr_ref)
     obj_spec_ref[...] = obj
     spec = spec_ref[...]
     o_re, o_im, s_re, s_im = obj[:, :LANES], obj[:, LANES:], spec[:, :LANES], spec[:, LANES:]
-    product = jnp.concatenate([o_re * s_re - o_im * s_im, -(o_re * s_im + o_im * s_re)], axis=1)
-    predicted = left(fl_ref, to_lanes(right(product, fr_ref)))
-    parts = []
-    for k in range(FK):
-        for c in range(PC):
-            usable = jnp.where(c < counts_ref[0], 1.0, 0.0).astype(F32)
-            lanes = slice(c * LANES, (c + 1) * LANES)
-            here = predicted[k * PP : (k + 1) * PP, lanes] * ((1 - 2 * k) / (PP * PP))
-            parts.append((here - windows[c] * cut(k + 1, c)) * usable)
-    residual = jnp.concatenate([jnp.concatenate(parts[k * PC : (k + 1) * PC], axis=1) for k in range(FK)], axis=0)
-    res = right(to_rows(left(fl_ref, residual)), fr_ref)
+    taken = [jnp.concatenate([windows[c] * cut(k + 1, c) for c in range(PC)], axis=1) for k in range(FK)]
+    data = right(to_rows(left(fl_ref, jnp.concatenate(taken, axis=0))), fr_ref)
+    product = jnp.concatenate([o_re * s_re - o_im * s_im, o_re * s_im + o_im * s_re], axis=1)
+    usable = [jnp.where(c < counts_ref[0, 0], 1.0, 0.0).astype(F32) for c in range(PC)]
+    difference = product - data
+    res = jnp.concatenate([difference[c * PP : (c + 1) * PP] * usable[c] for c in range(PC)], axis=0)
     res_spec_ref[...] = res
     r_re, r_im = res[:, :LANES], res[:, LANES:]
     back = jnp.concatenate([s_re * r_re + s_im * r_im, s_im * r_re - s_re * r_im], axis=1)
-    grad = left_part(fl_ref, to_lanes(right(back, fr_ref)))
+    grad = left(fl_ref[:PP, :], to_lanes(right(back, fr_ref)))
     for c in range(PC):
         mine = windows[c] * grad[:, c * LANES : (c + 1) * LANES] * (1.0 / (PP * PP))
         mine = pltpu.roll(jnp.concatenate([mine, jnp.zeros((TALL - PP, LANES), F32)], axis=0), row_rest[c], 0)
@@ -324,8 +317,8 @@
     grad_ref[...] = left(fl_ref, to_lanes(right(back, fr_ref)))
 
 
-def mode_kernel(grad_ref, field_ref, scale_ref, pupil_ref, bl_ref, br_ref, basis_hbm, out_ref, rows_scr, flat_ref, basis_scr, sems):
-    copies = fetch([(basis_hbm.at[:, pl.ds(j * CHUNK, CHUNK)], basis_scr.at[j]) for j in range(CHUNKS)], sems)
+def phase_grad_kernel(grad_ref, field_ref, scale_ref, pupil_ref, bl_ref, br_ref, basis_hbm, flat_ref, basis_ref, rows_scr, sems):
+    copies = fetch([(basis_hbm, basis_ref)], sems)
     re_parts, im_parts = [], []
     for n in range(NI):
         k, c = divmod(n, PC)
@@ -350,24 +343,23 @@
     slopes = crossed - pltpu.roll(crossed, 64, 1)
     for a in range(PU):
         flat_ref[:, a * PU : (a + 1) * PU] = slopes[a * NI : (a + 1) * NI, 0:PU]
-    flat_high, flat_low = split(flat_ref[...])
-    both = jnp.concatenate([flat_high, flat_low], axis=0)
+    copies[0].wait()
+
+
+def mode_kernel(flat_ref, basis_ref, out_ref):
+    high, low = split(flat_ref[...])
+    b_high, b_low = split(basis_ref[...])
 
     def by_modes(a, b):
         return lax.dot_general(a, b, (((1,), (1,)), ((), ())), preferred_element_type=F32)
 
-    out = jnp.zeros((NI, MODES), F32)
-    for j in range(CHUNKS):
-        copies[j].wait()
-        b_high, b_low = split(basis_scr[j])
-        lanes = slice(j * CHUNK, (j + 1) * CHUNK)
-        first = by_modes(both[:, lanes], b_high)
-        out = out + (first[:NI] + first[NI:] + by_modes(flat_high[:, lanes], b_low))
+    first = by_modes(jnp.concatenate([high, low], axis=0), b_high)
+    out = first[:NI] + first[NI:] + by_modes(high, b_low)
     out_ref[0, 0] = out[:PC]
     out_ref[1, 0] = out[PC:]
 
 
-def call(kernel, out_shapes, scratch=(), smem=0, near=0, far=0, name=None):
+def call(kernel, out_shapes, scratch=(), smem=0, near=0, far=0, aliases=None, name=None):
     vmem = pl.BlockSpec(memory_space=pltpu.VMEM)
     inner = pl.pallas_call(
         kernel,
@@ -375,6 +367,7 @@
         in_specs=[pl.BlockSpec(memory_space=pltpu.SMEM)] * smem + [vmem] * near + [pl.BlockSpec(memory_space=pltpu.HBM)] * far,
         out_specs=jax.tree.map(lambda _: vmem, out_shapes),
         scratch_shapes=list(scratch),
+        input_output_aliases=aliases or {},
         compiler_params=pltpu.CompilerParams(vmem_limit_bytes=VMEM_LIMIT),
         name=name,
     )
@@ -424,25 +417,34 @@
     const = {name: jnp.asarray(value) for name, value in host.items()}
     room = {name: like(value) for name, value in host.items()}
     halo_room = pltpu.VMEM((HALO, FK, columns), F32)
-    on_send, off_send = call(
-        pack_kernel, [shape(3 * HALO, columns)] * 2, scratch=[halo_room, halo_room, sems(4)], far=2, name="pack",
-    )(object_band, data_band)
+    pupil_room = [
+        pltpu.VMEM((CHUNKS, MODES, CHUNK), F32), pltpu.VMEM((NI, PU * PU), F32), pltpu.VMEM((FK, 1, PC, MODES), F32),
+        room["opening"], sems(CHUNKS + 2),
+    ]
+    wave_given = (coeffs, const["opening"], mode_basis)
+    early_matrices = ("pupil_right", "pupil_left", "fwd_left", "fwd_right")
+    matrices = [const[name] for name in early_matrices]
+    made_early = [shape(PU * NI, LANES)] + [room[name] for name in early_matrices]
+    on_send, off_send, *early = call(
+        pack_kernel, [shape(3 * HALO, columns)] * 2 + made_early,
+        scratch=[halo_room, halo_room, sems(4), sems(4)] + pupil_room, far=9, name="pack",
+    )(object_band, data_band, *wave_given, *matrices)
+    on_halo = swap_on(on_send)
     off_halo = swap_off(off_send)
-    on_halo = swap_on(on_send)
-    given = ("opening", "pupil_right", "pupil_left", "fwd_left", "fwd_right", "windows", "real_left", "back_left", "back_right")
-    kept = ("fwd_left", "fwd_right", "windows", "real_left", "back_left", "back_right")
-    pupil, field, spec, scale, ext, *kept_values = call(
+    kept = ("windows", "real_left", "back_left", "back_right")
+    pupil, _, _, fwd_left, fwd_right, field, spec, scale, ext, *kept_values = call(
         psf_kernel,
-        [shape(PU * NI, LANES), shape(2 * PP, NI * LANES), shape(PC * PP, 2 * LANES), shape(NI, LANES),
-         shape(1 + FK, HEIGHT, 4 * LANES)] + [room[name] for name in kept],
+        made_early + [shape(2 * PP, NI * LANES), shape(PC * PP, 2 * LANES), shape(NI, LANES), shape(1 + FK, HEIGHT, 4 * LANES)]
+        + [room[name] for name in kept],
         scratch=[
-            pltpu.VMEM((CHUNKS, MODES, CHUNK), F32), pltpu.VMEM((NI, PU * PU), F32), pltpu.VMEM((2, PU * NI, LANES), F32),
-            pltpu.VMEM((2 * PU, NI * LANES), F32), pltpu.VMEM((FK, 1, PC, MODES), F32), pltpu.VMEM((STRIDE, FK, columns), F32),
-            room["opening"], room["pupil_right"], room["pupil_left"], sems(CHUNKS + 12),
-        ],
+            pltpu.VMEM((2, PU * NI, LANES), F32), pltpu.VMEM((2 * PU, NI * LANES), F32), pltpu.VMEM((STRIDE, FK, columns), F32),
+            sems(6), sems(4),
+        ] + pupil_room,
+        near=5,
         far=13,
+        aliases={i: i for i in range(5)},
         name="psf",
-    )(coeffs, object_band, data_band, const["opening"], mode_basis, *[const[name] for name in given[1:]])
+    )(*early, *wave_given, object_band, data_band, *matrices, *[const[name] for name in kept])
     here = dict(zip(kept, kept_values))
     obj_spec, res_spec, centre, on_rim, off_rim = call(
         misfit_kernel,
@@ -452,13 +454,13 @@
         near=8,
         name="misfit",
     )(
-        jnp.transpose(offsets, (0, 2, 1)), window_ids, counts, on_halo, off_halo, spec, ext,
-        here["windows"], here["real_left"], here["fwd_left"], here["fwd_right"],
+        jnp.transpose(offsets, (0, 2, 1)), window_ids, counts.reshape(1, 1), on_halo, off_halo, spec, ext,
+        here["windows"], here["real_left"], fwd_left, fwd_right,
     )
     on_rim = swap_on(on_rim)
     off_rim = swap_off(off_rim)
     spread_grad = call(spread_grad_kernel, shape(2 * PP, PC * LANES), near=4, name="spread_grad")(
-        obj_spec, res_spec, here["fwd_left"], here["fwd_right"]
+        obj_spec, res_spec, fwd_left, fwd_right
     )
     even = lax.axis_index("patch") % 2 == 0
     upper = jnp.where(even, off_rim, on_rim)
@@ -466,17 +468,14 @@
     rows = jnp.concatenate([centre[:HALO] + upper, centre[HALO : STRIDE - HALO], centre[STRIDE - HALO :] + lower], axis=0)
     rows, spread_grad = lax.optimization_barrier((rows, spread_grad))
     moved = swap_frames(rows, 4)
-    coeff_grad = call(
-        mode_kernel, jax.ShapeDtypeStruct((FK, 1, PC, MODES), F32),
-        scratch=[
-            pltpu.VMEM((2, PU * NI, LANES), F32), pltpu.VMEM((NI, PU * PU), F32), pltpu.VMEM((CHUNKS, MODES, CHUNK), F32), sems(CHUNKS),
-        ],
-        near=6, far=1, name="modes",
+    flat, basis = call(
+        phase_grad_kernel, [shape(NI, PU * PU), shape(*mode_basis.shape)],
+        scratch=[pltpu.VMEM((2, PU * NI, LANES), F32), sems(1)], near=6, far=1, name="phase_grad",
     )(spread_grad, field, scale, pupil, here["back_left"], here["back_right"], mode_basis)
     rows = rows + moved
-    rows, coeff_grad = lax.optimization_barrier((rows, coeff_grad))
-    rows = rows + swap_frames(rows, 1)
-    rows = rows + swap_frames(rows, 2)
+    rows, flat = lax.optimization_barrier((rows, flat))
+    coeff_grad = call(mode_kernel, jax.ShapeDtypeStruct((FK, 1, PC, MODES), F32), near=2, name="modes")(flat, basis)
+    rows = rows + swap_frames(rows, 1) + swap_frames(rows, 2) + swap_frames(rows, 3)
     return rows, coeff_grad
 
 

time: 42.9 us -> 39.2 us (0.914)
  Pallas kernels: 13.1 us -> 10.5 us
  waiting for transfers between devices: 7.71 us -> 5.92 us
  starting transfers between devices: 19.6 us -> 20.4 us
    pallas_call x5 -> x6, Pallas kernels: 13.1 us -> 10.5 us  [run(): return inner(*placed)]
    ppermute x2, waiting for transfers between devices: 2.69 us -> 0.75 us  [swap_off(): return lax.ppermute(values, 'patch', pairs + [(j, i) for i, j in pairs])]
    ppermute x2, starting transfers between devices: 13.1 us -> 13.7 us  [swap_off(): return lax.ppermute(values, 'patch', pairs + [(j, i) for i, j in pairs])]
    ppermute x3 -> x4, starting transfers between devices: 6.33 us -> 6.49 us  [swap_frames(): return lax.ppermute(values, 'frames', [(i, i ^ bit) for i in range(count)])]
    ppermute x3 -> x4, waiting for transfers between devices: 5.01 us -> 5.16 us  [swap_frames(): return lax.ppermute(values, 'frames', [(i, i ^ bit) for i in range(count)])]
  transfers between devices with their start and end apart: 7 -> 8, of which waited for: 3 -> 5; matrix products, arithmetic and copies ran while one was open for 0% -> 0% of each run, Pallas kernels for 21% -> 14%
where the time goes in v2:
time: 39.2 us; the launch traced here: 38.9 us
  starting transfers between devices  20.4 us (52%)
  Pallas kernels  10.5 us (27%)
  waiting for transfers between devices  5.92 us (15%)
  between operations  1.41 us (4%)
  other arithmetic  0.67 us (2%)
    ppermute x2, starting transfers between devices, swap_off(): return lax.ppermute(values, 'patch', pairs + [(j, i) for i, j in pairs])  13.7 us
    pallas_call x6, Pallas kernels, run(): return inner(*placed)  10.5 us
    ppermute x4, starting transfers between devices, swap_frames(): return lax.ppermute(values, 'frames', [(i, i ^ bit) for i in range(count)])  6.49 us
    ppermute x4, waiting for transfers between devices, swap_frames(): return lax.ppermute(values, 'frames', [(i, i ^ bit) for i in range(count)])  5.16 us
  transfers between devices with their start and end apart: 8, of which 5 were waited for; matrix products, arithmetic and copies ran while one was open for 0% of the time, Pallas kernels for 14%

profile of v2, /device:TPU:6, one launch (start us, length us, event | category | flops | bytes accessed | tf_op | source)
XLA Modules:
  0.0 38.9 jit_solution(4623680718609666820)
XLA Ops:
  0.6 2.7 %pack.1 = (f32[72,256]{1,0:T(8,128)S(1)}, f32[72,256]{1,0:T(8,128)S(1)}, f32[384,128]{1,0:T(8,128)S(1)}, bf16[384,256]{1,0:T(8,128)(2,1)S(1)}, bf16[192,288]{1,0...) custom-call(f32[64,256]{1,0:T(8,128)} %object_hbm.3, f32[64,2,256]{2,1,0:T(2,128)} %data_hbm.3, ...), custom_call_target="tpu_custom_call" | custom-call | tf_op jit(solution)/shard_map/pack/pallas_call | solution.py:381
  3.3 0.1 collective-permute-start
  3.4 6.9 %collective-permute-start.1 = (f32[72,256]{1,0:T(8,128)S(1)}, f32[72,256]{1,0:T(8,128)S(1)}, u32[]{:S(2)}, u32[]{:S(2)}) collective-permute-start(f32[72,256]{1,0:T(8,128)S(1)} %get-tuple-element.32), channel_id=1, source_target_pairs={{1,2},{3,4},{5,6},{7,8},{9,10},{11,12},{13,14},{15,16},{17,18},{19... | collective-permute-start | bytes 221192 | tf_op jit(solution)/shard_map/ppermute | solution.py:406
  11.0 0.0 copy-start
  11.0 0.0 copy-start.1
  11.0 1.9 %psf.1 = (f32[384,128]{1,0:T(8,128)S(1)}, bf16[384,256]{1,0:T(8,128)(2,1)S(1)}, bf16[192,288]{1,0:T(8,128)(2,1)S(1)}, bf16[192,576]{1,0:T(8,128)(2,1)S(1)}, bf16...) custom-call(f32[384,128]{1,0:T(8,128)S(1)} %get-tuple-element.33.pup, ...), custom_call_target="tpu_custom_call", output_to_operand_aliasing={{0}: (0, {}), {1}: (1, {}), {2}: (2, {}), {3}: (3, {}), {4}... | custom-call | tf_op jit(solution)/shard_map/psf/pallas_call | solution.py:381
  12.9 0.0 collective-permute-done.on_ref
  12.9 0.1 collective-permute-done.1.off_ref
  13.0 0.0 copy-done
  13.0 0.0 copy-done.1
  13.0 2.4 %misfit.1 = (f32[384,256]{1,0:T(8,128)S(1)}, f32[384,256]{1,0:T(8,128)S(1)}, f32[64,256]{1,0:T(8,128)S(1)}, f32[24,256]{1,0:T(8,128)S(1)}, f32[24,256]{1,0:T(8,128)S(1)}) custom-call(s32[1,2,4]{2,1,0:T(2,128)S(1)} %bitcast.3, s32[1,4]{1,0:T(1,128)S(1)} %copy-done.1, s32[1,1]{1,0:T(1,128)} %bitcast.2.counts_ref, f32[72,256]{1,0:T(8,128)S(1)} %collective-permute-done.on_ref, ...), custom_call_target="tpu_custom_call" | custom-call | tf_op jit(solution)/shard_map/misfit/pallas_call | solution.py:381
  15.5 6.8 %collective-permute-start.2 = (f32[24,256]{1,0:T(8,128)S(1)}, f32[24,256]{1,0:T(8,128)S(1)}, u32[]{:S(2)}, u32[]{:S(2)}) collective-permute-start(f32[24,256]{1,0:T(8,128)S(1)} %get-tuple-element.45), channel_id=1, source_target_pairs={{1,2},{3,4},{5,6},{7,8},{9,10},{11,12},{13,14},{15,16},{17,18},{19... | collective-permute-start | bytes 73736 | tf_op jit(solution)/shard_map/ppermute | solution.py:406
  22.3 0.1 collective-permute-start.3
  22.4 0.8 %spread_grad.1.grad_ref = f32[192,512]{1,0:T(8,128)S(1)} custom-call(f32[384,256]{1,0:T(8,128)S(1)} %get-tuple-element.47.obj_spec_ref, f32[384,256]{1,0:T(8,128)S(1)} %get-tuple-element.48.res_spec_ref, bf16[192,576]{1,0:T(8,128)(2,1)S(1)} %get-tuple-element.42.fl_ref, bf16[768,256]{1,0:T(8,128)(2,1)S(1)} %get-tuple-element.43.fr_ref), custom_call_target="tpu_custom_call" | custom-call | tf_op jit(solution)/shard_map/spread_grad/pallas_call | solution.py:381
  23.2 0.6 %collective-permute-done.2 = f32[24,256]{1,0:T(8,128)S(1)} collective-permute-done((f32[24,256]{1,0:T(8,128)S(1)}, f32[24,256]{1,0:T(8,128)S(1)}, u32[]{:S(2)}, u32[]{:S(2)}) %collective-permute-start.2) | collective-permute-done | bytes 24608 | tf_op jit(solution)/shard_map/ppermute | solution.py:406
  23.9 0.0 collective-permute-done.3
  23.9 1.7 %collective-permute-start.4 = (f32[64,256]{1,0:T(8,128)S(1)}, f32[64,256]{1,0:T(8,128)S(1)}, u32[]{:S(2)}, u32[]{:S(2)}) collective-permute-start(f32[64,256]{1,0:T(8,128)S(1)} %pad_maximum_fusion), channel_id=1, source_target_pairs={{0,128},{32,160},{64,192},{96,224},{128,0},{160,32},{192,64},{224,... | collective-permute-start | bytes 196616 | tf_op jit(solution)/shard_map/ppermute | solution.py:411
  25.6 1.5 %phase_grad.1 = (f32[8,2304]{1,0:T(8,128)S(1)}, f32[200,2304]{1,0:T(8,128)S(1)}) custom-call(f32[192,512]{1,0:T(8,128)S(1)} %spread_grad.1.grad_ref, f32[192,1024]{1,0:T(8,128)S(1)} %get-tuple-element.51.field_ref, f32[8,128]{1,0:T(8,128)S(1)} %get-tuple-element.52.scale_ref, f32[384,128]{1,0:T(8,128)S(1)} %get-tuple-element.53.pupil_ref, ...), custom_call_target="tpu_custom_call" | custom-call | tf_op jit(solution)/shard_map/phase_grad/pallas_call | solution.py:381
  27.1 1.1 %collective-permute-done.4 = f32[64,256]{1,0:T(8,128)S(1)} collective-permute-done((f32[64,256]{1,0:T(8,128)S(1)}, f32[64,256]{1,0:T(8,128)S(1)}, u32[]{:S(2)}, u32[]{:S(2)}) %collective-permute-start.4) | collective-permute-done | bytes 65568 | tf_op jit(solution)/shard_map/ppermute | solution.py:411
  28.2 1.7 %collective-permute-start.5 = (f32[64,256]{1,0:T(8,128)S(1)}, f32[64,256]{1,0:T(8,128)S(1)}, u32[]{:S(2)}, u32[]{:S(2)}) collective-permute-start(f32[64,256]{1,0:T(8,128)S(1)} %add.25), channel_id=1, source_target_pairs={{0,32},{32,0},{64,96},{96,64},{128,160},{160,128},{192,224},{224,1... | collective-permute-start | bytes 196616 | tf_op jit(solution)/shard_map/ppermute | solution.py:411
  29.9 2.9 %collective-permute-start.6 = (f32[64,256]{1,0:T(8,128)S(1)}, f32[64,256]{1,0:T(8,128)S(1)}, u32[]{:S(2)}, u32[]{:S(2)}) collective-permute-start(f32[64,256]{1,0:T(8,128)S(1)} %add.25), channel_id=1, source_target_pairs={{0,64},{32,96},{64,0},{96,32},{128,192},{160,224},{192,128},{224,1... | collective-permute-start | bytes 196616 | tf_op jit(solution)/shard_map/ppermute | solution.py:411
  32.8 0.2 collective-permute-start.7
  33.0 1.2 %modes.1 = f32[2,1,4,200]{3,2,1,0:T(4,128)} custom-call(f32[8,2304]{1,0:T(8,128)S(1)} %get-tuple-element.58.flat_ref, f32[200,2304]{1,0:T(8,128)S(1)} %get-tuple-element.59.basis_ref), custom_call_target="tpu_custom_call" | custom-call | tf_op jit(solution)/shard_map/modes/pallas_call | solution.py:381
  34.3 0.0 collective-permute-done.5
  34.3 1.6 %collective-permute-done.6 = f32[64,256]{1,0:T(8,128)S(1)} collective-permute-done((f32[64,256]{1,0:T(8,128)S(1)}, f32[64,256]{1,0:T(8,128)S(1)}, u32[]{:S(2)}, u32[]{:S(2)}) %collective-permute-start.6) | collective-permute-done | bytes 65568 | tf_op jit(solution)/shard_map/ppermute | solution.py:411
  35.9 2.4 %collective-permute-done.7 = f32[64,256]{1,0:T(8,128)S(1)} collective-permute-done((f32[64,256]{1,0:T(8,128)S(1)}, f32[64,256]{1,0:T(8,128)S(1)}, u32[]{:S(2)}, u32[]{:S(2)}) %collective-permute-start.7) | collective-permute-done | bytes 65568 | tf_op jit(solution)/shard_map/ppermute | solution.py:411
  38.3 0.6 %add_add_fusion = f32[64,256]{1,0:T(8,128)} fusion(f32[64,256]{1,0:T(8,128)S(1)} %collective-permute-done.7, f32[64,256]{1,0:T(8,128)S(1)} %collective-permute-done.6, f32[64,256]{1,0:T(8,128)S(1)} %add.25, f32[64,256]{1,0:T(8,128)S(1)} %collective-permute-done.5), kind=kLoop, calls=%fused_computation.1 | loop fusion | flops 49152 | bytes 327680 | tf_op jit(solution)/shard_map/add | solution.py:478
  (4 shorter events, 0.0 us)
Async XLA Ops:
  3.3 9.6 %collective-permute-start = (f32[72,256]{1,0:T(8,128)S(1)}, f32[72,256]{1,0:T(8,128)S(1)}, u32[]{:S(2)}, u32[]{:S(2)}) collective-permute-start(f32[72,256]{1,0:T(8,128)S(1)} %get-tuple-element.31), channel_id=1, source_target_pairs={{0,1},{1,0},{2,3},{3,2},{4,5},{5,4},{6,7},{7,6},{8,9},{9,8},{10,11... | collective-permute-start | bytes 221192 | tf_op jit(solution)/shard_map/ppermute | solution.py:400
  3.4 9.6 %collective-permute-start.1 = (f32[72,256]{1,0:T(8,128)S(1)}, f32[72,256]{1,0:T(8,128)S(1)}, u32[]{:S(2)}, u32[]{:S(2)}) collective-permute-start(f32[72,256]{1,0:T(8,128)S(1)} %get-tuple-element.32), channel_id=1, source_target_pairs={{1,2},{3,4},{5,6},{7,8},{9,10},{11,12},{13,14},{15,16},{17,18},{19... | collective-permute-start | bytes 221192 | tf_op jit(solution)/shard_map/ppermute | solution.py:406
  11.0 2.0 %copy-start = (s32[1,4,2]{1,2,0:T(2,128)S(1)}, s32[1,4,2]{1,2,0:T(2,128)}, u32[]{:S(2)}) copy-start(s32[1,4,2]{1,2,0:T(2,128)} %param.20) | copy-start | bytes 100
  11.0 2.0 %copy-start.1 = (s32[1,4]{1,0:T(1,128)S(1)}, s32[1,4]{1,0:T(1,128)}, u32[]{:S(2)}) copy-start(s32[1,4]{1,0:T(1,128)} %kinds_ref.1) | copy-start | bytes 52
  15.5 8.4 %collective-permute-start.2 = (f32[24,256]{1,0:T(8,128)S(1)}, f32[24,256]{1,0:T(8,128)S(1)}, u32[]{:S(2)}, u32[]{:S(2)}) collective-permute-start(f32[24,256]{1,0:T(8,128)S(1)} %get-tuple-element.45), channel_id=1, source_target_pairs={{1,2},{3,4},{5,6},{7,8},{9,10},{11,12},{13,14},{15,16},{17,18},{19... | collective-permute-start | bytes 73736 | tf_op jit(solution)/shard_map/ppermute | solution.py:406
  22.3 1.6 %collective-permute-start.3 = (f32[24,256]{1,0:T(8,128)S(1)}, f32[24,256]{1,0:T(8,128)S(1)}, u32[]{:S(2)}, u32[]{:S(2)}) collective-permute-start(f32[24,256]{1,0:T(8,128)S(1)} %get-tuple-element.46), channel_id=1, source_target_pairs={{0,1},{1,0},{2,3},{3,2},{4,5},{5,4},{6,7},{7,6},{8,9},{9,8},{10,11... | collective-permute-start | bytes 73736 | tf_op jit(solution)/shard_map/ppermute | solution.py:400
  23.9 4.4 %collective-permute-start.4 = (f32[64,256]{1,0:T(8,128)S(1)}, f32[64,256]{1,0:T(8,128)S(1)}, u32[]{:S(2)}, u32[]{:S(2)}) collective-permute-start(f32[64,256]{1,0:T(8,128)S(1)} %pad_maximum_fusion), channel_id=1, source_target_pairs={{0,128},{32,160},{64,192},{96,224},{128,0},{160,32},{192,64},{224,... | collective-permute-start | bytes 196616 | tf_op jit(solution)/shard_map/ppermute | solution.py:411
  28.2 6.0 %collective-permute-start.5 = (f32[64,256]{1,0:T(8,128)S(1)}, f32[64,256]{1,0:T(8,128)S(1)}, u32[]{:S(2)}, u32[]{:S(2)}) collective-permute-start(f32[64,256]{1,0:T(8,128)S(1)} %add.25), channel_id=1, source_target_pairs={{0,32},{32,0},{64,96},{96,64},{128,160},{160,128},{192,224},{224,1... | collective-permute-start | bytes 196616 | tf_op jit(solution)/shard_map/ppermute | solution.py:411
  29.9 5.9 %collective-permute-start.6 = (f32[64,256]{1,0:T(8,128)S(1)}, f32[64,256]{1,0:T(8,128)S(1)}, u32[]{:S(2)}, u32[]{:S(2)}) collective-permute-start(f32[64,256]{1,0:T(8,128)S(1)} %add.25), channel_id=1, source_target_pairs={{0,64},{32,96},{64,0},{96,32},{128,192},{160,224},{192,128},{224,1... | collective-permute-start | bytes 196616 | tf_op jit(solution)/shard_map/ppermute | solution.py:411
  32.8 5.5 %collective-permute-start.7 = (f32[64,256]{1,0:T(8,128)S(1)}, f32[64,256]{1,0:T(8,128)S(1)}, u32[]{:S(2)}, u32[]{:S(2)}) collective-permute-start(f32[64,256]{1,0:T(8,128)S(1)} %add.25), channel_id=1, source_target_pairs={{0,96},{32,64},{64,32},{96,0},{128,224},{160,192},{192,160},{224,1... | collective-permute-start | bytes 196616 | tf_op jit(solution)/shard_map/ppermute | solution.py:411

commit v3 on v2

--- a/solution.py
+++ b/solution.py
@@ -107,15 +107,16 @@
 
 def to_rows(spectrum):
     parts = []
-    for c in range(PC):
+    for c in range(spectrum.shape[1] // LANES):
         lanes = slice(c * LANES, (c + 1) * LANES)
         parts.append(jnp.concatenate([spectrum[:PP, lanes], spectrum[PP:, lanes]], axis=1))
     return jnp.concatenate(parts, axis=0)
 
 
 def to_lanes(rows):
-    re = jnp.concatenate([rows[c * PP : (c + 1) * PP, :LANES] for c in range(PC)], axis=1)
-    im = jnp.concatenate([rows[c * PP : (c + 1) * PP, LANES:] for c in range(PC)], axis=1)
+    count = rows.shape[0] // PP
+    re = jnp.concatenate([rows[c * PP : (c + 1) * PP, :LANES] for c in range(count)], axis=1)
+    im = jnp.concatenate([rows[c * PP : (c + 1) * PP, LANES:] for c in range(count)], axis=1)
     return jnp.concatenate([re, im], axis=0)
 
 
@@ -147,13 +148,14 @@
     return lax.axis_index("patch") % 8 == 0
 
 
-def pupil_part(coeffs_hbm, opening_hbm, basis_hbm, pupil_ref, basis_scr, wave_scr, coeffs_ref, opening_ref, sems):
+def pupil_part(coeffs_hbm, opening_hbm, basis_hbm, pupil_ref, basis_scr, wave_scr, coeffs_ref, opening_ref, sems, later):
     copies = fetch(
         [(coeffs_hbm, coeffs_ref)]
         + [(basis_hbm.at[:, pl.ds(j * CHUNK, CHUNK)], basis_scr.at[j]) for j in range(CHUNKS)]
         + [(opening_hbm, opening_ref)],
         sems,
     )
+    late_copies = fetch(*later)
     pupil_ref[...] = jnp.zeros_like(pupil_ref)
     copies[0].wait()
     coeffs = jnp.concatenate([coeffs_ref[0, 0], coeffs_ref[1, 0]], axis=0)
@@ -180,6 +182,8 @@
     for a in range(PU):
         pupil_ref[a * NI : (a + 1) * NI, 0:PU] = re[:, a * PU : (a + 1) * PU]
         pupil_ref[a * NI : (a + 1) * NI, 64 : 64 + PU] = im[:, a * PU : (a + 1) * PU]
+    for copy in late_copies:
+        copy.wait()
 
 
 def pack_kernel(object_hbm, data_hbm, coeffs_hbm, opening_hbm, basis_hbm, pr_hbm, pl_hbm, fl_hbm, fr_hbm,
@@ -200,10 +204,8 @@
 
     @pl.when(is_early())
     def _():
-        matrices = fetch([(pr_hbm, pr_ref), (pl_hbm, pl_ref), (fl_hbm, fl_ref), (fr_hbm, fr_ref)], matrix_sems)
-        pupil_part(coeffs_hbm, opening_hbm, basis_hbm, pupil_ref, *scratch)
-        for copy in matrices:
-            copy.wait()
+        matrices = [(pr_hbm, pr_ref), (pl_hbm, pl_ref), (fl_hbm, fl_ref), (fr_hbm, fr_ref)]
+        pupil_part(coeffs_hbm, opening_hbm, basis_hbm, pupil_ref, *scratch, (matrices, matrix_sems))
 
     for copy in copies:
         copy.wait()
@@ -230,10 +232,8 @@
         ext[i, STRIDE + 2 * HALO :, LANES : 3 * LANES] = jnp.zeros((HEIGHT - STRIDE - 2 * HALO, 2 * LANES), F32)
     @pl.when(jnp.logical_not(is_early()))
     def _():
-        matrices = fetch([(pr_hbm, pr_ref), (pl_hbm, pl_ref), (fl_hbm, fl_ref), (fr_hbm, fr_ref)], matrix_sems)
-        pupil_part(coeffs_hbm, opening_hbm, basis_hbm, pupil_ref, *scratch)
-        for copy in matrices:
-            copy.wait()
+        matrices = [(pr_hbm, pr_ref), (pl_hbm, pl_ref), (fl_hbm, fl_ref), (fr_hbm, fr_ref)]
+        pupil_part(coeffs_hbm, opening_hbm, basis_hbm, pupil_ref, *scratch, (matrices, matrix_sems))
 
     mixed = right(pupil_ref[...], pr_ref)
     rows_scr[0] = mixed[:, :LANES]
@@ -261,7 +261,7 @@
         ext[k + 1, HALO : HALO + STRIDE, LANES : 3 * LANES] = data_scr[:, k, :]
 
 
-def misfit_kernel(offsets_ref, kinds_ref, counts_ref, on_ref, off_ref, spec_ref, ext_in, windows_ref, rl_ref, fl_ref, fr_ref,
+def misfit_kernel(offsets_ref, kinds_ref, counts_ref, off_ref, on_ref, spec_ref, ext_in, windows_ref, rl_ref, fl_ref, fr_ref,
                   obj_spec_ref, res_spec_ref, centre_ref, on_rim_ref, off_rim_ref, ext, total):
     even = lax.axis_index("patch") % 2 == 0
     on_at = pl.multiple_of(jnp.where(even, STRIDE + HALO, 0), 8)
@@ -283,22 +283,31 @@
         moved = pltpu.roll(block, 2 * LANES - shift[c], 1)[:, :LANES]
         return pltpu.roll(moved, jnp.where(row_rest[c] == 0, 0, TALL - row_rest[c]), 0)[:PP]
 
+    pairs = [(0, 1), (2, 3)]
     windows = [windows_ref[kinds_ref[0, c]] for c in range(PC)]
-    weighted = jnp.concatenate([windows[c] * cut(0, c) for c in range(PC)], axis=1)
-    obj = right(to_rows(left(rl_ref, weighted)), fr_ref)
-    obj_spec_ref[...] = obj
-    spec = spec_ref[...]
-    o_re, o_im, s_re, s_im = obj[:, :LANES], obj[:, LANES:], spec[:, :LANES], spec[:, LANES:]
-    taken = [jnp.concatenate([windows[c] * cut(k + 1, c) for c in range(PC)], axis=1) for k in range(FK)]
-    data = right(to_rows(left(fl_ref, jnp.concatenate(taken, axis=0))), fr_ref)
-    product = jnp.concatenate([o_re * s_re - o_im * s_im, o_re * s_im + o_im * s_re], axis=1)
-    usable = [jnp.where(c < counts_ref[0, 0], 1.0, 0.0).astype(F32) for c in range(PC)]
-    difference = product - data
-    res = jnp.concatenate([difference[c * PP : (c + 1) * PP] * usable[c] for c in range(PC)], axis=0)
-    res_spec_ref[...] = res
-    r_re, r_im = res[:, :LANES], res[:, LANES:]
-    back = jnp.concatenate([s_re * r_re + s_im * r_im, s_im * r_re - s_re * r_im], axis=1)
-    grad = left(fl_ref[:PP, :], to_lanes(right(back, fr_ref)))
+    weighted = [jnp.concatenate([windows[c] * cut(0, c) for c in pair], axis=1) for pair in pairs]
+    taken = [
+        jnp.concatenate([jnp.concatenate([windows[c] * cut(k + 1, c) for c in pair], axis=1) for k in range(FK)], axis=0)
+        for pair in pairs
+    ]
+    obj_left = [left(rl_ref, values) for values in weighted]
+    data_left = [left(fl_ref, values) for values in taken]
+    obj = [right(to_rows(values), fr_ref) for values in obj_left]
+    data = [right(to_rows(values), fr_ref) for values in data_left]
+    back = []
+    for g, pair in enumerate(pairs):
+        rows = slice(pair[0] * PP, (pair[-1] + 1) * PP)
+        obj_spec_ref[rows, :] = obj[g]
+        o_re, o_im, s_re, s_im = obj[g][:, :LANES], obj[g][:, LANES:], spec_ref[rows, :LANES], spec_ref[rows, LANES:]
+        product = jnp.concatenate([o_re * s_re - o_im * s_im, o_re * s_im + o_im * s_re], axis=1)
+        usable = [jnp.where(c < counts_ref[0, 0], 1.0, 0.0).astype(F32) for c in pair]
+        difference = product - data[g]
+        res = jnp.concatenate([difference[i * PP : (i + 1) * PP] * usable[i] for i in range(len(pair))], axis=0)
+        res_spec_ref[rows, :] = res
+        r_re, r_im = res[:, :LANES], res[:, LANES:]
+        back.append(jnp.concatenate([s_re * r_re + s_im * r_im, s_im * r_re - s_re * r_im], axis=1))
+    mixed = [to_lanes(right(values, fr_ref)) for values in back]
+    grad = jnp.concatenate([left(fl_ref[:PP, :], values) for values in mixed], axis=1)
     for c in range(PC):
         mine = windows[c] * grad[:, c * LANES : (c + 1) * LANES] * (1.0 / (PP * PP))
         mine = pltpu.roll(jnp.concatenate([mine, jnp.zeros((TALL - PP, LANES), F32)], axis=0), row_rest[c], 0)
@@ -454,7 +463,7 @@
         near=8,
         name="misfit",
     )(
-        jnp.transpose(offsets, (0, 2, 1)), window_ids, counts.reshape(1, 1), on_halo, off_halo, spec, ext,
+        jnp.transpose(offsets, (0, 2, 1)), window_ids, counts.reshape(1, 1), off_halo, on_halo, spec, ext,
         here["windows"], here["real_left"], fwd_left, fwd_right,
     )
     on_rim = swap_on(on_rim)
@@ -467,7 +476,7 @@
     lower = jnp.where(even, on_rim, off_rim)
     rows = jnp.concatenate([centre[:HALO] + upper, centre[HALO : STRIDE - HALO], centre[STRIDE - HALO :] + lower], axis=0)
     rows, spread_grad = lax.optimization_barrier((rows, spread_grad))
-    moved = swap_frames(rows, 4)
+    moved = swap_frames(rows, 5) + swap_frames(rows, 4) + swap_frames(rows, 1)
     flat, basis = call(
         phase_grad_kernel, [shape(NI, PU * PU), shape(*mode_basis.shape)],
         scratch=[pltpu.VMEM((2, PU * NI, LANES), F32), sems(1)], near=6, far=1, name="phase_grad",
@@ -475,7 +484,7 @@
     rows = rows + moved
     rows, flat = lax.optimization_barrier((rows, flat))
     coeff_grad = call(mode_kernel, jax.ShapeDtypeStruct((FK, 1, PC, MODES), F32), near=2, name="modes")(flat, basis)
-    rows = rows + swap_frames(rows, 1) + swap_frames(rows, 2) + swap_frames(rows, 3)
+    rows = rows + swap_frames(rows, 3)
     return rows, coeff_grad
 
 

time: 39.2 us -> 37 us (0.944)
  waiting for transfers between devices: 5.92 us -> 4.41 us
  starting transfers between devices: 20.4 us -> 19.8 us
    ppermute x4, waiting for transfers between devices: 5.16 us -> 3.83 us  [swap_frames(): return lax.ppermute(values, 'frames', [(i, i ^ bit) for i in range(count)])]
    ppermute x2, starting transfers between devices: 13.7 us -> 13.1 us  [swap_off(): return lax.ppermute(values, 'patch', pairs + [(j, i) for i, j in pairs])]
  transfers between devices with their start and end apart: 8 -> 8, of which waited for: 5 -> 5; matrix products, arithmetic and copies ran while one was open for 0% -> 0% of each run, Pallas kernels for 14% -> 15%
where the time goes in v3:
time: 37 us; the launch traced here: 36.7 us
  starting transfers between devices  19.8 us (54%)
  Pallas kernels  10.4 us (28%)
  waiting for transfers between devices  4.41 us (12%)
  between operations  1.41 us (4%)
  other arithmetic  0.68 us (2%)
    ppermute x2, starting transfers between devices, swap_off(): return lax.ppermute(values, 'patch', pairs + [(j, i) for i, j in pairs])  13.1 us
    pallas_call x6, Pallas kernels, run(): return inner(*placed)  10.4 us
    ppermute x4, starting transfers between devices, swap_frames(): return lax.ppermute(values, 'frames', [(i, i ^ bit) for i in range(count)])  6.57 us
    ppermute x4, waiting for transfers between devices, swap_frames(): return lax.ppermute(values, 'frames', [(i, i ^ bit) for i in range(count)])  3.83 us
  transfers between devices with their start and end apart: 8, of which 5 were waited for; matrix products, arithmetic and copies ran while one was open for 0% of the time, Pallas kernels for 15%

profile of v3, /device:TPU:6, one launch (start us, length us, event | category | flops | bytes accessed | tf_op | source)
XLA Modules:
  0.0 36.7 jit_solution(8477685512120488899)
XLA Ops:
  0.6 2.7 %pack.1 = (f32[72,256]{1,0:T(8,128)S(1)}, f32[72,256]{1,0:T(8,128)S(1)}, f32[384,128]{1,0:T(8,128)S(1)}, bf16[384,256]{1,0:T(8,128)(2,1)S(1)}, bf16[192,288]{1,0...) custom-call(f32[64,256]{1,0:T(8,128)} %object_hbm.3, f32[64,2,256]{2,1,0:T(2,128)} %data_hbm.3, ...), custom_call_target="tpu_custom_call" | custom-call | tf_op jit(solution)/shard_map/pack/pallas_call | solution.py:390
  3.3 6.3 %collective-permute-start = (f32[72,256]{1,0:T(8,128)S(1)}, f32[72,256]{1,0:T(8,128)S(1)}, u32[]{:S(2)}, u32[]{:S(2)}) collective-permute-start(f32[72,256]{1,0:T(8,128)S(1)} %get-tuple-element.31), channel_id=1, source_target_pairs={{1,2},{3,4},{5,6},{7,8},{9,10},{11,12},{13,14},{15,16},{17,18},{19... | collective-permute-start | bytes 221192 | tf_op jit(solution)/shard_map/ppermute | solution.py:415
  9.6 0.1 collective-permute-start.1
  10.3 0.0 copy-start
  10.3 0.0 copy-start.1
  10.4 1.9 %psf.1 = (f32[384,128]{1,0:T(8,128)S(1)}, bf16[384,256]{1,0:T(8,128)(2,1)S(1)}, bf16[192,288]{1,0:T(8,128)(2,1)S(1)}, bf16[192,576]{1,0:T(8,128)(2,1)S(1)}, bf16...) custom-call(f32[384,128]{1,0:T(8,128)S(1)} %get-tuple-element.33.pup, ...), custom_call_target="tpu_custom_call", output_to_operand_aliasing={{0}: (0, {}), {1}: (1, {}), {2}: (2, {}), {3}: (3, {}), {4}... | custom-call | tf_op jit(solution)/shard_map/psf/pallas_call | solution.py:390
  12.2 0.0 collective-permute-done.off_ref
  12.3 0.0 collective-permute-done.1.on_ref
  12.3 0.0 copy-done
  12.3 0.0 copy-done.1
  12.3 2.3 %misfit.1 = (f32[384,256]{1,0:T(8,128)S(1)}, f32[384,256]{1,0:T(8,128)S(1)}, f32[64,256]{1,0:T(8,128)S(1)}, f32[24,256]{1,0:T(8,128)S(1)}, f32[24,256]{1,0:T(8,128)S(1)}) custom-call(s32[1,2,4]{2,1,0:T(2,128)S(1)} %bitcast.3, s32[1,4]{1,0:T(1,128)S(1)} %copy-done.1, s32[1,1]{1,0:T(1,128)} %bitcast.2.counts_ref, f32[72,256]{1,0:T(8,128)S(1)} %collective-permute-done.off_ref, ...), custom_call_target="tpu_custom_call" | custom-call | tf_op jit(solution)/shard_map/misfit/pallas_call | solution.py:390
  14.6 6.8 %collective-permute-start.2 = (f32[24,256]{1,0:T(8,128)S(1)}, f32[24,256]{1,0:T(8,128)S(1)}, u32[]{:S(2)}, u32[]{:S(2)}) collective-permute-start(f32[24,256]{1,0:T(8,128)S(1)} %get-tuple-element.45), channel_id=1, source_target_pairs={{1,2},{3,4},{5,6},{7,8},{9,10},{11,12},{13,14},{15,16},{17,18},{19... | collective-permute-start | bytes 73736 | tf_op jit(solution)/shard_map/ppermute | solution.py:415
  21.4 0.1 collective-permute-start.3
  21.5 0.8 %spread_grad.1.grad_ref = f32[192,512]{1,0:T(8,128)S(1)} custom-call(f32[384,256]{1,0:T(8,128)S(1)} %get-tuple-element.47.obj_spec_ref, f32[384,256]{1,0:T(8,128)S(1)} %get-tuple-element.48.res_spec_ref, bf16[192,576]{1,0:T(8,128)(2,1)S(1)} %get-tuple-element.42.fl_ref, bf16[768,256]{1,0:T(8,128)(2,1)S(1)} %get-tuple-element.43.fr_ref), custom_call_target="tpu_custom_call" | custom-call | tf_op jit(solution)/shard_map/spread_grad/pallas_call | solution.py:390
  22.3 0.5 %collective-permute-done.2 = f32[24,256]{1,0:T(8,128)S(1)} collective-permute-done((f32[24,256]{1,0:T(8,128)S(1)}, f32[24,256]{1,0:T(8,128)S(1)}, u32[]{:S(2)}, u32[]{:S(2)}) %collective-permute-start.2) | collective-permute-done | bytes 24608 | tf_op jit(solution)/shard_map/ppermute | solution.py:415
  22.9 0.0 collective-permute-done.3
  22.9 3.0 %collective-permute-start.4 = (f32[64,256]{1,0:T(8,128)S(1)}, f32[64,256]{1,0:T(8,128)S(1)}, u32[]{:S(2)}, u32[]{:S(2)}) collective-permute-start(f32[64,256]{1,0:T(8,128)S(1)} %pad_maximum_fusion), channel_id=1, source_target_pairs={{0,160},{32,128},{64,224},{96,192},{128,32},{160,0},{192,96},{224,... | collective-permute-start | bytes 196616 | tf_op jit(solution)/shard_map/ppermute | solution.py:420
  25.9 0.1 collective-permute-start.5
  26.0 0.6 %collective-permute-start.6 = (f32[64,256]{1,0:T(8,128)S(1)}, f32[64,256]{1,0:T(8,128)S(1)}, u32[]{:S(2)}, u32[]{:S(2)}) collective-permute-start(f32[64,256]{1,0:T(8,128)S(1)} %pad_maximum_fusion), channel_id=1, source_target_pairs={{0,32},{32,0},{64,96},{96,64},{128,160},{160,128},{192,224},{224,1... | collective-permute-start | bytes 196616 | tf_op jit(solution)/shard_map/ppermute | solution.py:420
  26.6 1.5 %phase_grad.1 = (f32[8,2304]{1,0:T(8,128)S(1)}, f32[200,2304]{1,0:T(8,128)S(1)}) custom-call(f32[192,512]{1,0:T(8,128)S(1)} %spread_grad.1.grad_ref, f32[192,1024]{1,0:T(8,128)S(1)} %get-tuple-element.51.field_ref, f32[8,128]{1,0:T(8,128)S(1)} %get-tuple-element.52.scale_ref, f32[384,128]{1,0:T(8,128)S(1)} %get-tuple-element.53.pupil_ref, ...), custom_call_target="tpu_custom_call" | custom-call | tf_op jit(solution)/shard_map/phase_grad/pallas_call | solution.py:390
  28.1 0.8 %collective-permute-done.4 = f32[64,256]{1,0:T(8,128)S(1)} collective-permute-done((f32[64,256]{1,0:T(8,128)S(1)}, f32[64,256]{1,0:T(8,128)S(1)}, u32[]{:S(2)}, u32[]{:S(2)}) %collective-permute-start.4) | collective-permute-done | bytes 65568 | tf_op jit(solution)/shard_map/ppermute | solution.py:420
  28.9 1.5 %collective-permute-done.5 = f32[64,256]{1,0:T(8,128)S(1)} collective-permute-done((f32[64,256]{1,0:T(8,128)S(1)}, f32[64,256]{1,0:T(8,128)S(1)}, u32[]{:S(2)}, u32[]{:S(2)}) %collective-permute-start.5) | collective-permute-done | bytes 65568 | tf_op jit(solution)/shard_map/ppermute | solution.py:420
  30.4 0.1 collective-permute-done.6
  30.5 2.9 %collective-permute-start.7 = (f32[64,256]{1,0:T(8,128)S(1)}, f32[64,256]{1,0:T(8,128)S(1)}, u32[]{:S(2)}, u32[]{:S(2)}) collective-permute-start(f32[64,256]{1,0:T(8,128)S(1)} %add_add_fusion), channel_id=1, source_target_pairs={{0,96},{32,64},{64,32},{96,0},{128,224},{160,192},{192,160},{224,1... | collective-permute-start | bytes 196616 | tf_op jit(solution)/shard_map/ppermute | solution.py:420
  33.4 1.2 %modes.1 = f32[2,1,4,200]{3,2,1,0:T(4,128)} custom-call(f32[8,2304]{1,0:T(8,128)S(1)} %get-tuple-element.58.flat_ref, f32[200,2304]{1,0:T(8,128)S(1)} %get-tuple-element.59.basis_ref), custom_call_target="tpu_custom_call" | custom-call | tf_op jit(solution)/shard_map/modes/pallas_call | solution.py:390
  34.6 1.5 %collective-permute-done.7 = f32[64,256]{1,0:T(8,128)S(1)} collective-permute-done((f32[64,256]{1,0:T(8,128)S(1)}, f32[64,256]{1,0:T(8,128)S(1)}, u32[]{:S(2)}, u32[]{:S(2)}) %collective-permute-start.7) | collective-permute-done | bytes 65568 | tf_op jit(solution)/shard_map/ppermute | solution.py:420
  36.1 0.6 %add.28 = f32[64,256]{1,0:T(8,128)} add(f32[64,256]{1,0:T(8,128)S(1)} %add_add_fusion, f32[64,256]{1,0:T(8,128)S(1)} %collective-permute-done.7) | non-fusion elementwise | flops 16384 | bytes 196608 | tf_op jit(solution)/shard_map/add | solution.py:487
  (4 shorter events, 0.0 us)
Async XLA Ops:
  3.3 9.0 %collective-permute-start = (f32[72,256]{1,0:T(8,128)S(1)}, f32[72,256]{1,0:T(8,128)S(1)}, u32[]{:S(2)}, u32[]{:S(2)}) collective-permute-start(f32[72,256]{1,0:T(8,128)S(1)} %get-tuple-element.31), channel_id=1, source_target_pairs={{1,2},{3,4},{5,6},{7,8},{9,10},{11,12},{13,14},{15,16},{17,18},{19... | collective-permute-start | bytes 221192 | tf_op jit(solution)/shard_map/ppermute | solution.py:415
  9.6 2.7 %collective-permute-start.1 = (f32[72,256]{1,0:T(8,128)S(1)}, f32[72,256]{1,0:T(8,128)S(1)}, u32[]{:S(2)}, u32[]{:S(2)}) collective-permute-start(f32[72,256]{1,0:T(8,128)S(1)} %get-tuple-element.32), channel_id=1, source_target_pairs={{0,1},{1,0},{2,3},{3,2},{4,5},{5,4},{6,7},{7,6},{8,9},{9,8},{10,11... | collective-permute-start | bytes 221192 | tf_op jit(solution)/shard_map/ppermute | solution.py:409
  10.3 1.9 %copy-start = (s32[1,4,2]{1,2,0:T(2,128)S(1)}, s32[1,4,2]{1,2,0:T(2,128)}, u32[]{:S(2)}) copy-start(s32[1,4,2]{1,2,0:T(2,128)} %param.20) | copy-start | bytes 100
  10.3 1.9 %copy-start.1 = (s32[1,4]{1,0:T(1,128)S(1)}, s32[1,4]{1,0:T(1,128)}, u32[]{:S(2)}) copy-start(s32[1,4]{1,0:T(1,128)} %kinds_ref.1) | copy-start | bytes 52
  14.6 8.3 %collective-permute-start.2 = (f32[24,256]{1,0:T(8,128)S(1)}, f32[24,256]{1,0:T(8,128)S(1)}, u32[]{:S(2)}, u32[]{:S(2)}) collective-permute-start(f32[24,256]{1,0:T(8,128)S(1)} %get-tuple-element.45), channel_id=1, source_target_pairs={{1,2},{3,4},{5,6},{7,8},{9,10},{11,12},{13,14},{15,16},{17,18},{19... | collective-permute-start | bytes 73736 | tf_op jit(solution)/shard_map/ppermute | solution.py:415
  21.4 1.5 %collective-permute-start.3 = (f32[24,256]{1,0:T(8,128)S(1)}, f32[24,256]{1,0:T(8,128)S(1)}, u32[]{:S(2)}, u32[]{:S(2)}) collective-permute-start(f32[24,256]{1,0:T(8,128)S(1)} %get-tuple-element.46), channel_id=1, source_target_pairs={{0,1},{1,0},{2,3},{3,2},{4,5},{5,4},{6,7},{7,6},{8,9},{9,8},{10,11... | collective-permute-start | bytes 73736 | tf_op jit(solution)/shard_map/ppermute | solution.py:409
  22.9 6.0 %collective-permute-start.4 = (f32[64,256]{1,0:T(8,128)S(1)}, f32[64,256]{1,0:T(8,128)S(1)}, u32[]{:S(2)}, u32[]{:S(2)}) collective-permute-start(f32[64,256]{1,0:T(8,128)S(1)} %pad_maximum_fusion), channel_id=1, source_target_pairs={{0,160},{32,128},{64,224},{96,192},{128,32},{160,0},{192,96},{224,... | collective-permute-start | bytes 196616 | tf_op jit(solution)/shard_map/ppermute | solution.py:420
  25.9 4.4 %collective-permute-start.5 = (f32[64,256]{1,0:T(8,128)S(1)}, f32[64,256]{1,0:T(8,128)S(1)}, u32[]{:S(2)}, u32[]{:S(2)}) collective-permute-start(f32[64,256]{1,0:T(8,128)S(1)} %pad_maximum_fusion), channel_id=1, source_target_pairs={{0,128},{32,160},{64,192},{96,224},{128,0},{160,32},{192,64},{224,... | collective-permute-start | bytes 196616 | tf_op jit(solution)/shard_map/ppermute | solution.py:420
  26.0 4.4 %collective-permute-start.6 = (f32[64,256]{1,0:T(8,128)S(1)}, f32[64,256]{1,0:T(8,128)S(1)}, u32[]{:S(2)}, u32[]{:S(2)}) collective-permute-start(f32[64,256]{1,0:T(8,128)S(1)} %pad_maximum_fusion), channel_id=1, source_target_pairs={{0,32},{32,0},{64,96},{96,64},{128,160},{160,128},{192,224},{224,1... | collective-permute-start | bytes 196616 | tf_op jit(solution)/shard_map/ppermute | solution.py:420
  30.5 5.6 %collective-permute-start.7 = (f32[64,256]{1,0:T(8,128)S(1)}, f32[64,256]{1,0:T(8,128)S(1)}, u32[]{:S(2)}, u32[]{:S(2)}) collective-permute-start(f32[64,256]{1,0:T(8,128)S(1)} %add_add_fusion), channel_id=1, source_target_pairs={{0,96},{32,64},{64,32},{96,0},{128,224},{160,192},{192,160},{224,1... | collective-permute-start | bytes 196616 | tf_op jit(solution)/shard_map/ppermute | solution.py:420

commit v4 on v3

--- a/solution.py
+++ b/solution.py
@@ -186,8 +186,8 @@
         copy.wait()
 
 
-def pack_kernel(object_hbm, data_hbm, coeffs_hbm, opening_hbm, basis_hbm, pr_hbm, pl_hbm, fl_hbm, fr_hbm,
-                on_ref, off_ref, pupil_ref, pr_ref, pl_ref, fl_ref, fr_ref, on_scr, off_scr, send_sems, matrix_sems, *scratch):
+def pack_kernel(object_hbm, data_hbm, coeffs_hbm, opening_hbm, basis_hbm, pr_hbm, pl_hbm,
+                on_ref, off_ref, pupil_ref, pr_ref, pl_ref, on_scr, off_scr, send_sems, matrix_sems, *scratch):
     even = lax.axis_index("patch") % 2 == 0
     low, high = STRIDE - HALO, 0
     on_at = pl.multiple_of(jnp.where(even, low, high), 8)
@@ -204,7 +204,7 @@
 
     @pl.when(is_early())
     def _():
-        matrices = [(pr_hbm, pr_ref), (pl_hbm, pl_ref), (fl_hbm, fl_ref), (fr_hbm, fr_ref)]
+        matrices = [(pr_hbm, pr_ref), (pl_hbm, pl_ref)]
         pupil_part(coeffs_hbm, opening_hbm, basis_hbm, pupil_ref, *scratch, (matrices, matrix_sems))
 
     for copy in copies:
@@ -215,12 +215,13 @@
         on_ref[rows, :] = on_scr[:, k, :]
 
 
-def psf_kernel(pupil_in, pr_in, pl_in, fl_in, fr_in, coeffs_hbm, opening_hbm, basis_hbm, object_hbm, data_hbm, pr_hbm, pl_hbm, fl_hbm, fr_hbm,
+def psf_kernel(pupil_in, pr_in, pl_in, coeffs_hbm, opening_hbm, basis_hbm, object_hbm, data_hbm, pr_hbm, pl_hbm, fl_hbm, fr_hbm,
                windows_hbm, rl_hbm, bl_hbm, br_hbm,
                pupil_ref, pr_ref, pl_ref, fl_ref, fr_ref, field_ref, spec_ref, scale_ref, ext, windows_ref, rl_ref, bl_ref, br_ref,
                rows_scr, left_scr, data_scr, sems, matrix_sems, *scratch):
     copies = fetch(
         [
+            (fl_hbm, fl_ref), (fr_hbm, fr_ref),
             (object_hbm, ext.at[0, pl.ds(HALO, STRIDE), pl.ds(LANES, 2 * LANES)]),
             (data_hbm, data_scr), (windows_hbm, windows_ref), (rl_hbm, rl_ref), (bl_hbm, bl_ref), (br_hbm, br_ref),
         ],
@@ -232,7 +233,7 @@
         ext[i, STRIDE + 2 * HALO :, LANES : 3 * LANES] = jnp.zeros((HEIGHT - STRIDE - 2 * HALO, 2 * LANES), F32)
     @pl.when(jnp.logical_not(is_early()))
     def _():
-        matrices = [(pr_hbm, pr_ref), (pl_hbm, pl_ref), (fl_hbm, fl_ref), (fr_hbm, fr_ref)]
+        matrices = [(pr_hbm, pr_ref), (pl_hbm, pl_ref)]
         pupil_part(coeffs_hbm, opening_hbm, basis_hbm, pupil_ref, *scratch, (matrices, matrix_sems))
 
     mixed = right(pupil_ref[...], pr_ref)
@@ -254,8 +255,13 @@
         [intensity[:, n * LANES : (n + 1) * LANES] * scale[n : n + 1, :] for n in range(NI)], axis=1
     )
     pair = jnp.concatenate([spread[:, : PC * LANES], spread[:, PC * LANES :]], axis=0)
-    spec_ref[...] = right(to_rows(left(fl_ref, pair)), fr_ref)
-    for copy in copies:
+    copies[0].wait()
+    copies[1].wait()
+    half = PC // 2 * LANES
+    mixed = [left(fl_ref, pair[:, g * half : (g + 1) * half]) for g in range(2)]
+    spectra = [right(to_rows(values), fr_ref) for values in mixed]
+    spec_ref[...] = jnp.concatenate(spectra, axis=0)
+    for copy in copies[2:]:
         copy.wait()
     for k in range(FK):
         ext[k + 1, HALO : HALO + STRIDE, LANES : 3 * LANES] = data_scr[:, k, :]
@@ -433,25 +439,25 @@
     wave_given = (coeffs, const["opening"], mode_basis)
     early_matrices = ("pupil_right", "pupil_left", "fwd_left", "fwd_right")
     matrices = [const[name] for name in early_matrices]
-    made_early = [shape(PU * NI, LANES)] + [room[name] for name in early_matrices]
+    made_early = [shape(PU * NI, LANES)] + [room[name] for name in early_matrices[:2]]
     on_send, off_send, *early = call(
         pack_kernel, [shape(3 * HALO, columns)] * 2 + made_early,
-        scratch=[halo_room, halo_room, sems(4), sems(4)] + pupil_room, far=9, name="pack",
-    )(object_band, data_band, *wave_given, *matrices)
+        scratch=[halo_room, halo_room, sems(4), sems(4)] + pupil_room, far=7, name="pack",
+    )(object_band, data_band, *wave_given, *matrices[:2])
     on_halo = swap_on(on_send)
     off_halo = swap_off(off_send)
     kept = ("windows", "real_left", "back_left", "back_right")
     pupil, _, _, fwd_left, fwd_right, field, spec, scale, ext, *kept_values = call(
         psf_kernel,
-        made_early + [shape(2 * PP, NI * LANES), shape(PC * PP, 2 * LANES), shape(NI, LANES), shape(1 + FK, HEIGHT, 4 * LANES)]
+        made_early + [room[name] for name in early_matrices[2:]] + [shape(2 * PP, NI * LANES), shape(PC * PP, 2 * LANES), shape(NI, LANES), shape(1 + FK, HEIGHT, 4 * LANES)]
         + [room[name] for name in kept],
         scratch=[
             pltpu.VMEM((2, PU * NI, LANES), F32), pltpu.VMEM((2 * PU, NI * LANES), F32), pltpu.VMEM((STRIDE, FK, columns), F32),
-            sems(6), sems(4),
+            sems(8), sems(4),
         ] + pupil_room,
-        near=5,
+        near=3,
         far=13,
-        aliases={i: i for i in range(5)},
+        aliases={i: i for i in range(3)},
         name="psf",
     )(*early, *wave_given, object_band, data_band, *matrices, *[const[name] for name in kept])
     here = dict(zip(kept, kept_values))

time: 37 us -> 36.8 us (level)
  no operation moved by 1% of the time
where the time goes in v4:
time: 36.8 us; the launch traced here: 36.5 us
  starting transfers between devices  19.9 us (54%)
  Pallas kernels  10.3 us (28%)
  waiting for transfers between devices  4.27 us (12%)
  between operations  1.43 us (4%)
  other arithmetic  0.68 us (2%)
    ppermute x2, starting transfers between devices, swap_off(): return lax.ppermute(values, 'patch', pairs + [(j, i) for i, j in pairs])  13.2 us
    pallas_call x6, Pallas kernels, run(): return inner(*placed)  10.3 us
    ppermute x4, starting transfers between devices, swap_frames(): return lax.ppermute(values, 'frames', [(i, i ^ bit) for i in range(count)])  6.5 us
    ppermute x4, waiting for transfers between devices, swap_frames(): return lax.ppermute(values, 'frames', [(i, i ^ bit) for i in range(count)])  3.73 us
  transfers between devices with their start and end apart: 8, of which 5 were waited for; matrix products, arithmetic and copies ran while one was open for 0% of the time, Pallas kernels for 15%

profile of v4, /device:TPU:6, one launch (start us, length us, event | category | flops | bytes accessed | tf_op | source)
XLA Modules:
  0.0 36.5 jit_solution(4733526520265351798)
XLA Ops:
  0.6 2.5 %pack.1 = (f32[72,256]{1,0:T(8,128)S(1)}, f32[72,256]{1,0:T(8,128)S(1)}, f32[384,128]{1,0:T(8,128)S(1)}, bf16[384,256]{1,0:T(8,128)(2,1)S(1)}, bf16[192,288]{1,0:T(8,128)(2,1)S(1)}) custom-call(f32[64,256]{1,0:T(8,128)} %object_hbm.3, f32[64,2,256]{2,1,0:T(2,128)} %data_hbm.3, f32[2,1,4,200]{3,2,1,0:T(4,128)} %coeffs_hbm.3, ...), custom_call_target="tpu_custom_call" | custom-call | tf_op jit(solution)/shard_map/pack/pallas_call | solution.py:396
  3.1 6.5 %collective-permute-start = (f32[72,256]{1,0:T(8,128)S(1)}, f32[72,256]{1,0:T(8,128)S(1)}, u32[]{:S(2)}, u32[]{:S(2)}) collective-permute-start(f32[72,256]{1,0:T(8,128)S(1)} %get-tuple-element.29), channel_id=1, source_target_pairs={{1,2},{3,4},{5,6},{7,8},{9,10},{11,12},{13,14},{15,16},{17,18},{19... | collective-permute-start | bytes 221192 | tf_op jit(solution)/shard_map/ppermute | solution.py:421
  9.6 0.1 collective-permute-start.1
  10.3 0.0 copy-start
  10.3 0.0 copy-start.1
  10.4 1.9 %psf.1 = (f32[384,128]{1,0:T(8,128)S(1)}, bf16[384,256]{1,0:T(8,128)(2,1)S(1)}, bf16[192,288]{1,0:T(8,128)(2,1)S(1)}, bf16[192,576]{1,0:T(8,128)(2,1)S(1)}, bf16...) custom-call(f32[384,128]{1,0:T(8,128)S(1)} %get-tuple-element.31.pup, ...), custom_call_target="tpu_custom_call", output_to_operand_aliasing={{0}: (0, {}), {1}: (1, {}), {2}: (2, {})} | custom-call | tf_op jit(solution)/shard_map/psf/pallas_call | solution.py:396
  12.3 0.0 collective-permute-done.off_ref
  12.3 0.0 collective-permute-done.1.on_ref
  12.3 0.0 copy-done
  12.3 0.0 copy-done.1
  12.4 2.3 %misfit.1 = (f32[384,256]{1,0:T(8,128)S(1)}, f32[384,256]{1,0:T(8,128)S(1)}, f32[64,256]{1,0:T(8,128)S(1)}, f32[24,256]{1,0:T(8,128)S(1)}, f32[24,256]{1,0:T(8,128)S(1)}) custom-call(s32[1,2,4]{2,1,0:T(2,128)S(1)} %bitcast.3, s32[1,4]{1,0:T(1,128)S(1)} %copy-done.1, s32[1,1]{1,0:T(1,128)} %bitcast.2.counts_ref, f32[72,256]{1,0:T(8,128)S(1)} %collective-permute-done.off_ref, ...), custom_call_target="tpu_custom_call" | custom-call | tf_op jit(solution)/shard_map/misfit/pallas_call | solution.py:396
  14.7 6.7 %collective-permute-start.2 = (f32[24,256]{1,0:T(8,128)S(1)}, f32[24,256]{1,0:T(8,128)S(1)}, u32[]{:S(2)}, u32[]{:S(2)}) collective-permute-start(f32[24,256]{1,0:T(8,128)S(1)} %get-tuple-element.41), channel_id=1, source_target_pairs={{1,2},{3,4},{5,6},{7,8},{9,10},{11,12},{13,14},{15,16},{17,18},{19... | collective-permute-start | bytes 73736 | tf_op jit(solution)/shard_map/ppermute | solution.py:421
  21.4 0.1 collective-permute-start.3
  21.5 0.8 %spread_grad.1.grad_ref = f32[192,512]{1,0:T(8,128)S(1)} custom-call(f32[384,256]{1,0:T(8,128)S(1)} %get-tuple-element.43.obj_spec_ref, f32[384,256]{1,0:T(8,128)S(1)} %get-tuple-element.44.res_spec_ref, bf16[192,576]{1,0:T(8,128)(2,1)S(1)} %get-tuple-element.38.fl_ref, bf16[768,256]{1,0:T(8,128)(2,1)S(1)} %get-tuple-element.39.fr_ref), custom_call_target="tpu_custom_call" | custom-call | tf_op jit(solution)/shard_map/spread_grad/pallas_call | solution.py:396
  22.3 0.5 %collective-permute-done.2 = f32[24,256]{1,0:T(8,128)S(1)} collective-permute-done((f32[24,256]{1,0:T(8,128)S(1)}, f32[24,256]{1,0:T(8,128)S(1)}, u32[]{:S(2)}, u32[]{:S(2)}) %collective-permute-start.2) | collective-permute-done | bytes 24608 | tf_op jit(solution)/shard_map/ppermute | solution.py:421
  22.9 0.0 collective-permute-done.3
  22.9 2.9 %collective-permute-start.4 = (f32[64,256]{1,0:T(8,128)S(1)}, f32[64,256]{1,0:T(8,128)S(1)}, u32[]{:S(2)}, u32[]{:S(2)}) collective-permute-start(f32[64,256]{1,0:T(8,128)S(1)} %pad_maximum_fusion), channel_id=1, source_target_pairs={{0,160},{32,128},{64,224},{96,192},{128,32},{160,0},{192,96},{224,... | collective-permute-start | bytes 196616 | tf_op jit(solution)/shard_map/ppermute | solution.py:426
  25.8 0.2 collective-permute-start.5
  26.0 0.4 %collective-permute-start.6 = (f32[64,256]{1,0:T(8,128)S(1)}, f32[64,256]{1,0:T(8,128)S(1)}, u32[]{:S(2)}, u32[]{:S(2)}) collective-permute-start(f32[64,256]{1,0:T(8,128)S(1)} %pad_maximum_fusion), channel_id=1, source_target_pairs={{0,32},{32,0},{64,96},{96,64},{128,160},{160,128},{192,224},{224,1... | collective-permute-start | bytes 196616 | tf_op jit(solution)/shard_map/ppermute | solution.py:426
  26.5 1.5 %phase_grad.1 = (f32[8,2304]{1,0:T(8,128)S(1)}, f32[200,2304]{1,0:T(8,128)S(1)}) custom-call(f32[192,512]{1,0:T(8,128)S(1)} %spread_grad.1.grad_ref, f32[192,1024]{1,0:T(8,128)S(1)} %get-tuple-element.47.field_ref, f32[8,128]{1,0:T(8,128)S(1)} %get-tuple-element.48.scale_ref, f32[384,128]{1,0:T(8,128)S(1)} %get-tuple-element.49.pupil_ref, ...), custom_call_target="tpu_custom_call" | custom-call | tf_op jit(solution)/shard_map/phase_grad/pallas_call | solution.py:396
  28.0 0.9 %collective-permute-done.4 = f32[64,256]{1,0:T(8,128)S(1)} collective-permute-done((f32[64,256]{1,0:T(8,128)S(1)}, f32[64,256]{1,0:T(8,128)S(1)}, u32[]{:S(2)}, u32[]{:S(2)}) %collective-permute-start.4) | collective-permute-done | bytes 65568 | tf_op jit(solution)/shard_map/ppermute | solution.py:426
  28.9 1.4 %collective-permute-done.5 = f32[64,256]{1,0:T(8,128)S(1)} collective-permute-done((f32[64,256]{1,0:T(8,128)S(1)}, f32[64,256]{1,0:T(8,128)S(1)}, u32[]{:S(2)}, u32[]{:S(2)}) %collective-permute-start.5) | collective-permute-done | bytes 65568 | tf_op jit(solution)/shard_map/ppermute | solution.py:426
  30.2 0.1 collective-permute-done.6
  30.3 2.9 %collective-permute-start.7 = (f32[64,256]{1,0:T(8,128)S(1)}, f32[64,256]{1,0:T(8,128)S(1)}, u32[]{:S(2)}, u32[]{:S(2)}) collective-permute-start(f32[64,256]{1,0:T(8,128)S(1)} %add_add_fusion), channel_id=1, source_target_pairs={{0,96},{32,64},{64,32},{96,0},{128,224},{160,192},{192,160},{224,1... | collective-permute-start | bytes 196616 | tf_op jit(solution)/shard_map/ppermute | solution.py:426
  33.2 1.2 %modes.1 = f32[2,1,4,200]{3,2,1,0:T(4,128)} custom-call(f32[8,2304]{1,0:T(8,128)S(1)} %get-tuple-element.54.flat_ref, f32[200,2304]{1,0:T(8,128)S(1)} %get-tuple-element.55.basis_ref), custom_call_target="tpu_custom_call" | custom-call | tf_op jit(solution)/shard_map/modes/pallas_call | solution.py:396
  34.5 1.4 %collective-permute-done.7 = f32[64,256]{1,0:T(8,128)S(1)} collective-permute-done((f32[64,256]{1,0:T(8,128)S(1)}, f32[64,256]{1,0:T(8,128)S(1)}, u32[]{:S(2)}, u32[]{:S(2)}) %collective-permute-start.7) | collective-permute-done | bytes 65568 | tf_op jit(solution)/shard_map/ppermute | solution.py:426
  35.9 0.6 %add.28 = f32[64,256]{1,0:T(8,128)} add(f32[64,256]{1,0:T(8,128)S(1)} %add_add_fusion, f32[64,256]{1,0:T(8,128)S(1)} %collective-permute-done.7) | non-fusion elementwise | flops 16384 | bytes 196608 | tf_op jit(solution)/shard_map/add | solution.py:493
  (4 shorter events, 0.0 us)
Async XLA Ops:
  3.1 9.2 %collective-permute-start = (f32[72,256]{1,0:T(8,128)S(1)}, f32[72,256]{1,0:T(8,128)S(1)}, u32[]{:S(2)}, u32[]{:S(2)}) collective-permute-start(f32[72,256]{1,0:T(8,128)S(1)} %get-tuple-element.29), channel_id=1, source_target_pairs={{1,2},{3,4},{5,6},{7,8},{9,10},{11,12},{13,14},{15,16},{17,18},{19... | collective-permute-start | bytes 221192 | tf_op jit(solution)/shard_map/ppermute | solution.py:421
  9.6 2.7 %collective-permute-start.1 = (f32[72,256]{1,0:T(8,128)S(1)}, f32[72,256]{1,0:T(8,128)S(1)}, u32[]{:S(2)}, u32[]{:S(2)}) collective-permute-start(f32[72,256]{1,0:T(8,128)S(1)} %get-tuple-element.30), channel_id=1, source_target_pairs={{0,1},{1,0},{2,3},{3,2},{4,5},{5,4},{6,7},{7,6},{8,9},{9,8},{10,11... | collective-permute-start | bytes 221192 | tf_op jit(solution)/shard_map/ppermute | solution.py:415
  10.3 2.0 %copy-start = (s32[1,4,2]{1,2,0:T(2,128)S(1)}, s32[1,4,2]{1,2,0:T(2,128)}, u32[]{:S(2)}) copy-start(s32[1,4,2]{1,2,0:T(2,128)} %param.20) | copy-start | bytes 100
  10.3 2.0 %copy-start.1 = (s32[1,4]{1,0:T(1,128)S(1)}, s32[1,4]{1,0:T(1,128)}, u32[]{:S(2)}) copy-start(s32[1,4]{1,0:T(1,128)} %kinds_ref.1) | copy-start | bytes 52
  14.7 8.2 %collective-permute-start.2 = (f32[24,256]{1,0:T(8,128)S(1)}, f32[24,256]{1,0:T(8,128)S(1)}, u32[]{:S(2)}, u32[]{:S(2)}) collective-permute-start(f32[24,256]{1,0:T(8,128)S(1)} %get-tuple-element.41), channel_id=1, source_target_pairs={{1,2},{3,4},{5,6},{7,8},{9,10},{11,12},{13,14},{15,16},{17,18},{19... | collective-permute-start | bytes 73736 | tf_op jit(solution)/shard_map/ppermute | solution.py:421
  21.4 1.5 %collective-permute-start.3 = (f32[24,256]{1,0:T(8,128)S(1)}, f32[24,256]{1,0:T(8,128)S(1)}, u32[]{:S(2)}, u32[]{:S(2)}) collective-permute-start(f32[24,256]{1,0:T(8,128)S(1)} %get-tuple-element.42), channel_id=1, source_target_pairs={{0,1},{1,0},{2,3},{3,2},{4,5},{5,4},{6,7},{7,6},{8,9},{9,8},{10,11... | collective-permute-start | bytes 73736 | tf_op jit(solution)/shard_map/ppermute | solution.py:415
  22.9 6.0 %collective-permute-start.4 = (f32[64,256]{1,0:T(8,128)S(1)}, f32[64,256]{1,0:T(8,128)S(1)}, u32[]{:S(2)}, u32[]{:S(2)}) collective-permute-start(f32[64,256]{1,0:T(8,128)S(1)} %pad_maximum_fusion), channel_id=1, source_target_pairs={{0,160},{32,128},{64,224},{96,192},{128,32},{160,0},{192,96},{224,... | collective-permute-start | bytes 196616 | tf_op jit(solution)/shard_map/ppermute | solution.py:426
  25.8 4.4 %collective-permute-start.5 = (f32[64,256]{1,0:T(8,128)S(1)}, f32[64,256]{1,0:T(8,128)S(1)}, u32[]{:S(2)}, u32[]{:S(2)}) collective-permute-start(f32[64,256]{1,0:T(8,128)S(1)} %pad_maximum_fusion), channel_id=1, source_target_pairs={{0,128},{32,160},{64,192},{96,224},{128,0},{160,32},{192,64},{224,... | collective-permute-start | bytes 196616 | tf_op jit(solution)/shard_map/ppermute | solution.py:426
  26.0 4.3 %collective-permute-start.6 = (f32[64,256]{1,0:T(8,128)S(1)}, f32[64,256]{1,0:T(8,128)S(1)}, u32[]{:S(2)}, u32[]{:S(2)}) collective-permute-start(f32[64,256]{1,0:T(8,128)S(1)} %pad_maximum_fusion), channel_id=1, source_target_pairs={{0,32},{32,0},{64,96},{96,64},{128,160},{160,128},{192,224},{224,1... | collective-permute-start | bytes 196616 | tf_op jit(solution)/shard_map/ppermute | solution.py:426
  30.3 5.6 %collective-permute-start.7 = (f32[64,256]{1,0:T(8,128)S(1)}, f32[64,256]{1,0:T(8,128)S(1)}, u32[]{:S(2)}, u32[]{:S(2)}) collective-permute-start(f32[64,256]{1,0:T(8,128)S(1)} %add_add_fusion), channel_id=1, source_target_pairs={{0,96},{32,64},{64,32},{96,0},{128,224},{160,192},{192,160},{224,1... | collective-permute-start | bytes 196616 | tf_op jit(solution)/shard_map/ppermute | solution.py:426

commit v5 on v4

--- a/solution.py
+++ b/solution.py
@@ -243,7 +243,8 @@
         lanes = slice(n * LANES, (n + 1) * LANES)
         left_scr[0:PU, lanes] = rows_scr[0, pl.ds(n, PU, stride=NI), :]
         left_scr[PU:, lanes] = rows_scr[1, pl.ds(n, PU, stride=NI), :]
-    field = left(pl_ref, left_scr[...])
+    count = NI // 2 * LANES
+    field = jnp.concatenate([left(pl_ref, left_scr[:, g * count : (g + 1) * count]) for g in range(2)], axis=1)
     field_ref[...] = field
     intensity = field[:PP] * field[:PP] + field[PP:] * field[PP:]
     sums = jnp.concatenate(

time: 36.8 us -> 36.8 us (level)
  no operation moved by 1% of the time
where the time goes in v5:
time: 36.8 us; the launch traced here: 36.5 us
  starting transfers between devices  19.9 us (54%)
  Pallas kernels  10.3 us (28%)
  waiting for transfers between devices  4.27 us (12%)
  between operations  1.43 us (4%)
  other arithmetic  0.68 us (2%)
    ppermute x2, starting transfers between devices, swap_off(): return lax.ppermute(values, 'patch', pairs + [(j, i) for i, j in pairs])  13.2 us
    pallas_call x6, Pallas kernels, run(): return inner(*placed)  10.3 us
    ppermute x4, starting transfers between devices, swap_frames(): return lax.ppermute(values, 'frames', [(i, i ^ bit) for i in range(count)])  6.5 us
    ppermute x4, waiting for transfers between devices, swap_frames(): return lax.ppermute(values, 'frames', [(i, i ^ bit) for i in range(count)])  3.73 us
  transfers between devices with their start and end apart: 8, of which 5 were waited for; matrix products, arithmetic and copies ran while one was open for 0% of the time, Pallas kernels for 15%

profile of v5, /device:TPU:6, one launch (start us, length us, event | category | flops | bytes accessed | tf_op | source)
XLA Modules:
  0.0 36.5 jit_solution(4733526520265351798)
XLA Ops:
  0.6 2.5 %pack.1 = (f32[72,256]{1,0:T(8,128)S(1)}, f32[72,256]{1,0:T(8,128)S(1)}, f32[384,128]{1,0:T(8,128)S(1)}, bf16[384,256]{1,0:T(8,128)(2,1)S(1)}, bf16[192,288]{1,0:T(8,128)(2,1)S(1)}) custom-call(f32[64,256]{1,0:T(8,128)} %object_hbm.3, f32[64,2,256]{2,1,0:T(2,128)} %data_hbm.3, f32[2,1,4,200]{3,2,1,0:T(4,128)} %coeffs_hbm.3, ...), custom_call_target="tpu_custom_call" | custom-call | tf_op jit(solution)/shard_map/pack/pallas_call | solution.py:397
  3.1 6.5 %collective-permute-start = (f32[72,256]{1,0:T(8,128)S(1)}, f32[72,256]{1,0:T(8,128)S(1)}, u32[]{:S(2)}, u32[]{:S(2)}) collective-permute-start(f32[72,256]{1,0:T(8,128)S(1)} %get-tuple-element.29), channel_id=1, source_target_pairs={{1,2},{3,4},{5,6},{7,8},{9,10},{11,12},{13,14},{15,16},{17,18},{19... | collective-permute-start | bytes 221192 | tf_op jit(solution)/shard_map/ppermute | solution.py:422
  9.6 0.1 collective-permute-start.1
  10.3 0.0 copy-start
  10.3 0.0 copy-start.1
  10.4 1.9 %psf.1 = (f32[384,128]{1,0:T(8,128)S(1)}, bf16[384,256]{1,0:T(8,128)(2,1)S(1)}, bf16[192,288]{1,0:T(8,128)(2,1)S(1)}, bf16[192,576]{1,0:T(8,128)(2,1)S(1)}, bf16...) custom-call(f32[384,128]{1,0:T(8,128)S(1)} %get-tuple-element.31.pup, ...), custom_call_target="tpu_custom_call", output_to_operand_aliasing={{0}: (0, {}), {1}: (1, {}), {2}: (2, {})} | custom-call | tf_op jit(solution)/shard_map/psf/pallas_call | solution.py:397
  12.3 0.0 collective-permute-done.off_ref
  12.3 0.0 collective-permute-done.1.on_ref
  12.3 0.0 copy-done
  12.3 0.0 copy-done.1
  12.4 2.3 %misfit.1 = (f32[384,256]{1,0:T(8,128)S(1)}, f32[384,256]{1,0:T(8,128)S(1)}, f32[64,256]{1,0:T(8,128)S(1)}, f32[24,256]{1,0:T(8,128)S(1)}, f32[24,256]{1,0:T(8,128)S(1)}) custom-call(s32[1,2,4]{2,1,0:T(2,128)S(1)} %bitcast.3, s32[1,4]{1,0:T(1,128)S(1)} %copy-done.1, s32[1,1]{1,0:T(1,128)} %bitcast.2.counts_ref, f32[72,256]{1,0:T(8,128)S(1)} %collective-permute-done.off_ref, ...), custom_call_target="tpu_custom_call" | custom-call | tf_op jit(solution)/shard_map/misfit/pallas_call | solution.py:397
  14.7 6.7 %collective-permute-start.2 = (f32[24,256]{1,0:T(8,128)S(1)}, f32[24,256]{1,0:T(8,128)S(1)}, u32[]{:S(2)}, u32[]{:S(2)}) collective-permute-start(f32[24,256]{1,0:T(8,128)S(1)} %get-tuple-element.41), channel_id=1, source_target_pairs={{1,2},{3,4},{5,6},{7,8},{9,10},{11,12},{13,14},{15,16},{17,18},{19... | collective-permute-start | bytes 73736 | tf_op jit(solution)/shard_map/ppermute | solution.py:422
  21.4 0.1 collective-permute-start.3
  21.5 0.8 %spread_grad.1.grad_ref = f32[192,512]{1,0:T(8,128)S(1)} custom-call(f32[384,256]{1,0:T(8,128)S(1)} %get-tuple-element.43.obj_spec_ref, f32[384,256]{1,0:T(8,128)S(1)} %get-tuple-element.44.res_spec_ref, bf16[192,576]{1,0:T(8,128)(2,1)S(1)} %get-tuple-element.38.fl_ref, bf16[768,256]{1,0:T(8,128)(2,1)S(1)} %get-tuple-element.39.fr_ref), custom_call_target="tpu_custom_call" | custom-call | tf_op jit(solution)/shard_map/spread_grad/pallas_call | solution.py:397
  22.3 0.5 %collective-permute-done.2 = f32[24,256]{1,0:T(8,128)S(1)} collective-permute-done((f32[24,256]{1,0:T(8,128)S(1)}, f32[24,256]{1,0:T(8,128)S(1)}, u32[]{:S(2)}, u32[]{:S(2)}) %collective-permute-start.2) | collective-permute-done | bytes 24608 | tf_op jit(solution)/shard_map/ppermute | solution.py:422
  22.9 0.0 collective-permute-done.3
  22.9 2.9 %collective-permute-start.4 = (f32[64,256]{1,0:T(8,128)S(1)}, f32[64,256]{1,0:T(8,128)S(1)}, u32[]{:S(2)}, u32[]{:S(2)}) collective-permute-start(f32[64,256]{1,0:T(8,128)S(1)} %pad_maximum_fusion), channel_id=1, source_target_pairs={{0,160},{32,128},{64,224},{96,192},{128,32},{160,0},{192,96},{224,... | collective-permute-start | bytes 196616 | tf_op jit(solution)/shard_map/ppermute | solution.py:427
  25.8 0.2 collective-permute-start.5
  26.0 0.4 %collective-permute-start.6 = (f32[64,256]{1,0:T(8,128)S(1)}, f32[64,256]{1,0:T(8,128)S(1)}, u32[]{:S(2)}, u32[]{:S(2)}) collective-permute-start(f32[64,256]{1,0:T(8,128)S(1)} %pad_maximum_fusion), channel_id=1, source_target_pairs={{0,32},{32,0},{64,96},{96,64},{128,160},{160,128},{192,224},{224,1... | collective-permute-start | bytes 196616 | tf_op jit(solution)/shard_map/ppermute | solution.py:427
  26.5 1.5 %phase_grad.1 = (f32[8,2304]{1,0:T(8,128)S(1)}, f32[200,2304]{1,0:T(8,128)S(1)}) custom-call(f32[192,512]{1,0:T(8,128)S(1)} %spread_grad.1.grad_ref, f32[192,1024]{1,0:T(8,128)S(1)} %get-tuple-element.47.field_ref, f32[8,128]{1,0:T(8,128)S(1)} %get-tuple-element.48.scale_ref, f32[384,128]{1,0:T(8,128)S(1)} %get-tuple-element.49.pupil_ref, ...), custom_call_target="tpu_custom_call" | custom-call | tf_op jit(solution)/shard_map/phase_grad/pallas_call | solution.py:397
  28.0 0.9 %collective-permute-done.4 = f32[64,256]{1,0:T(8,128)S(1)} collective-permute-done((f32[64,256]{1,0:T(8,128)S(1)}, f32[64,256]{1,0:T(8,128)S(1)}, u32[]{:S(2)}, u32[]{:S(2)}) %collective-permute-start.4) | collective-permute-done | bytes 65568 | tf_op jit(solution)/shard_map/ppermute | solution.py:427
  28.9 1.4 %collective-permute-done.5 = f32[64,256]{1,0:T(8,128)S(1)} collective-permute-done((f32[64,256]{1,0:T(8,128)S(1)}, f32[64,256]{1,0:T(8,128)S(1)}, u32[]{:S(2)}, u32[]{:S(2)}) %collective-permute-start.5) | collective-permute-done | bytes 65568 | tf_op jit(solution)/shard_map/ppermute | solution.py:427
  30.2 0.1 collective-permute-done.6
  30.3 2.9 %collective-permute-start.7 = (f32[64,256]{1,0:T(8,128)S(1)}, f32[64,256]{1,0:T(8,128)S(1)}, u32[]{:S(2)}, u32[]{:S(2)}) collective-permute-start(f32[64,256]{1,0:T(8,128)S(1)} %add_add_fusion), channel_id=1, source_target_pairs={{0,96},{32,64},{64,32},{96,0},{128,224},{160,192},{192,160},{224,1... | collective-permute-start | bytes 196616 | tf_op jit(solution)/shard_map/ppermute | solution.py:427
  33.2 1.2 %modes.1 = f32[2,1,4,200]{3,2,1,0:T(4,128)} custom-call(f32[8,2304]{1,0:T(8,128)S(1)} %get-tuple-element.54.flat_ref, f32[200,2304]{1,0:T(8,128)S(1)} %get-tuple-element.55.basis_ref), custom_call_target="tpu_custom_call" | custom-call | tf_op jit(solution)/shard_map/modes/pallas_call | solution.py:397
  34.5 1.4 %collective-permute-done.7 = f32[64,256]{1,0:T(8,128)S(1)} collective-permute-done((f32[64,256]{1,0:T(8,128)S(1)}, f32[64,256]{1,0:T(8,128)S(1)}, u32[]{:S(2)}, u32[]{:S(2)}) %collective-permute-start.7) | collective-permute-done | bytes 65568 | tf_op jit(solution)/shard_map/ppermute | solution.py:427
  35.9 0.6 %add.28 = f32[64,256]{1,0:T(8,128)} add(f32[64,256]{1,0:T(8,128)S(1)} %add_add_fusion, f32[64,256]{1,0:T(8,128)S(1)} %collective-permute-done.7) | non-fusion elementwise | flops 16384 | bytes 196608 | tf_op jit(solution)/shard_map/add | solution.py:494
  (4 shorter events, 0.0 us)
Async XLA Ops:
  3.1 9.2 %collective-permute-start = (f32[72,256]{1,0:T(8,128)S(1)}, f32[72,256]{1,0:T(8,128)S(1)}, u32[]{:S(2)}, u32[]{:S(2)}) collective-permute-start(f32[72,256]{1,0:T(8,128)S(1)} %get-tuple-element.29), channel_id=1, source_target_pairs={{1,2},{3,4},{5,6},{7,8},{9,10},{11,12},{13,14},{15,16},{17,18},{19... | collective-permute-start | bytes 221192 | tf_op jit(solution)/shard_map/ppermute | solution.py:422
  9.6 2.7 %collective-permute-start.1 = (f32[72,256]{1,0:T(8,128)S(1)}, f32[72,256]{1,0:T(8,128)S(1)}, u32[]{:S(2)}, u32[]{:S(2)}) collective-permute-start(f32[72,256]{1,0:T(8,128)S(1)} %get-tuple-element.30), channel_id=1, source_target_pairs={{0,1},{1,0},{2,3},{3,2},{4,5},{5,4},{6,7},{7,6},{8,9},{9,8},{10,11... | collective-permute-start | bytes 221192 | tf_op jit(solution)/shard_map/ppermute | solution.py:416
  10.3 2.0 %copy-start = (s32[1,4,2]{1,2,0:T(2,128)S(1)}, s32[1,4,2]{1,2,0:T(2,128)}, u32[]{:S(2)}) copy-start(s32[1,4,2]{1,2,0:T(2,128)} %param.20) | copy-start | bytes 100
  10.3 2.0 %copy-start.1 = (s32[1,4]{1,0:T(1,128)S(1)}, s32[1,4]{1,0:T(1,128)}, u32[]{:S(2)}) copy-start(s32[1,4]{1,0:T(1,128)} %kinds_ref.1) | copy-start | bytes 52
  14.7 8.2 %collective-permute-start.2 = (f32[24,256]{1,0:T(8,128)S(1)}, f32[24,256]{1,0:T(8,128)S(1)}, u32[]{:S(2)}, u32[]{:S(2)}) collective-permute-start(f32[24,256]{1,0:T(8,128)S(1)} %get-tuple-element.41), channel_id=1, source_target_pairs={{1,2},{3,4},{5,6},{7,8},{9,10},{11,12},{13,14},{15,16},{17,18},{19... | collective-permute-start | bytes 73736 | tf_op jit(solution)/shard_map/ppermute | solution.py:422
  21.4 1.5 %collective-permute-start.3 = (f32[24,256]{1,0:T(8,128)S(1)}, f32[24,256]{1,0:T(8,128)S(1)}, u32[]{:S(2)}, u32[]{:S(2)}) collective-permute-start(f32[24,256]{1,0:T(8,128)S(1)} %get-tuple-element.42), channel_id=1, source_target_pairs={{0,1},{1,0},{2,3},{3,2},{4,5},{5,4},{6,7},{7,6},{8,9},{9,8},{10,11... | collective-permute-start | bytes 73736 | tf_op jit(solution)/shard_map/ppermute | solution.py:416
  22.9 6.0 %collective-permute-start.4 = (f32[64,256]{1,0:T(8,128)S(1)}, f32[64,256]{1,0:T(8,128)S(1)}, u32[]{:S(2)}, u32[]{:S(2)}) collective-permute-start(f32[64,256]{1,0:T(8,128)S(1)} %pad_maximum_fusion), channel_id=1, source_target_pairs={{0,160},{32,128},{64,224},{96,192},{128,32},{160,0},{192,96},{224,... | collective-permute-start | bytes 196616 | tf_op jit(solution)/shard_map/ppermute | solution.py:427
  25.8 4.4 %collective-permute-start.5 = (f32[64,256]{1,0:T(8,128)S(1)}, f32[64,256]{1,0:T(8,128)S(1)}, u32[]{:S(2)}, u32[]{:S(2)}) collective-permute-start(f32[64,256]{1,0:T(8,128)S(1)} %pad_maximum_fusion), channel_id=1, source_target_pairs={{0,128},{32,160},{64,192},{96,224},{128,0},{160,32},{192,64},{224,... | collective-permute-start | bytes 196616 | tf_op jit(solution)/shard_map/ppermute | solution.py:427
  26.0 4.3 %collective-permute-start.6 = (f32[64,256]{1,0:T(8,128)S(1)}, f32[64,256]{1,0:T(8,128)S(1)}, u32[]{:S(2)}, u32[]{:S(2)}) collective-permute-start(f32[64,256]{1,0:T(8,128)S(1)} %pad_maximum_fusion), channel_id=1, source_target_pairs={{0,32},{32,0},{64,96},{96,64},{128,160},{160,128},{192,224},{224,1... | collective-permute-start | bytes 196616 | tf_op jit(solution)/shard_map/ppermute | solution.py:427
  30.3 5.6 %collective-permute-start.7 = (f32[64,256]{1,0:T(8,128)S(1)}, f32[64,256]{1,0:T(8,128)S(1)}, u32[]{:S(2)}, u32[]{:S(2)}) collective-permute-start(f32[64,256]{1,0:T(8,128)S(1)} %add_add_fusion), channel_id=1, source_target_pairs={{0,96},{32,64},{64,32},{96,0},{128,224},{160,192},{192,160},{224,1... | collective-permute-start | bytes 196616 | tf_op jit(solution)/shard_map/ppermute | solution.py:427
